TPU v7x, 32 devices: a whole 2x2x4 slice. The times are simulated.
32 devices in a mesh: row: 4 (over x, core), col: 8 (over z, y).
Axes of the slice: x: 2, y: 2, z: 4, core: 2. Of those that a mesh axis runs over, the one named last changes fastest.
Arguments:
- left_tiles: bfloat16 [4, 8, 6, 128, 128], P('row', 'col'), may hold values from -6 to 6
- left_index: int32 [4, 8, 6], replicated, may hold values from 0 to 16, as said below
- right_tiles: bfloat16 [4, 8, 2, 3, 128, 128], P('row', 'col'), may hold values from -0.125 to 0.125
- right_index: int32 [4, 8, 2, 3], replicated, may hold values from 0 to 8, as said below
Outputs:
- product: bfloat16 [1024, 1024], P('row', 'col')
Inputs may be any that keep to these rules, and one draw needn't show every extreme that they name: `left_index`: in each block r, c the used slots come first and name distinct positions i * 8 + k; unused slots hold 16. Every block uses at least a third of its 6 slots, some block uses all of them and some block leaves slots unused. `right_index`: in each half block r, c, h the used slots come first and name distinct positions k + j; unused slots hold 8. Every half block uses at least a third of its 3 slots, some uses all of them and some leaves slots unused.
All inputs are finite; a program needn't handle non-finite values.
Results may differ from a plain program's by a relative error of at most 0.001.
Values may be sent and summed in bfloat16 or wider, within the bound.
No kernel may reach another device: no remote copies, remote signals or barrier semaphores. Data moves between devices by JAX's collectives and lax.ppermute only.
A program may use at most 64 MiB of HBM per device.

v0:
```python
import jax
import jax.numpy as jnp
from jax import lax
from jax.experimental import pallas as pl
from jax.experimental.pallas import tpu as pltpu
from jax.sharding import PartitionSpec as P

KT = 8
RT = 2
BITS = 15
LEAST = 100
PAD = 16
SIDES = 4
FLOPS = 10**10
SMEM = pl.BlockSpec(memory_space=pltpu.SMEM)
VMEM = pl.BlockSpec(memory_space=pltpu.VMEM)


def position():
    col = lax.axis_index("col")
    return lax.axis_index("row"), col >> 1, col & 1


def find_matches(left_index, right_index):
    slots = left_index.shape[-1]
    inner, _, _, right_slots = right_index.shape
    left_index = left_index.transpose(2, 0, 1)
    right_index = right_index.transpose(0, 3, 2, 1)

    def kernel(li_ref, ri_ref, codes_ref):
        row, z, y = position()

        @pl.loop(0, inner // 2)
        def _(n):
            zp = z ^ (2 * n)
            for side in range(SIDES):
                column = 2 * (z ^ (side >> 1)) + (y ^ (side & 1))
                have = [ri_ref[zp, t, y, column] for t in range(right_slots)]
                for slot in range(slots):
                    at = li_ref[slot, row, 2 * zp + y]
                    k = lax.rem(at, KT)
                    first = 1 + lax.div(at, KT) * right_slots
                    code = jnp.int32(0)
                    for t in range(right_slots):
                        code = jnp.where(have[t] == k, first + t, code)
                    codes_ref[(n * SIDES + side) * slots + slot] = jnp.where(at < RT * KT, code, 0)

    return pl.pallas_call(
        kernel,
        out_shape=jax.ShapeDtypeStruct((inner // 2 * SIDES * slots,), jnp.int32),
        in_specs=[SMEM] * 2,
        out_specs=SMEM,
    )(left_index, right_index)


def add_block(codes_ref, n, side, left_ref, right_at, right_slots, total_ref):
    slots, tile, _ = left_ref.shape

    @pl.loop(0, slots)
    def _(slot):
        code = codes_ref[(n * SIDES + side) * slots + slot]

        @pl.when(code > 0)
        def _():
            i = lax.div(code - 1, right_slots)
            rows = pl.ds(pl.multiple_of(i * tile, tile), tile)
            total_ref[rows, :] += jnp.dot(
                left_ref[slot],
                right_at(lax.rem(code - 1, right_slots)),
                preferred_element_type=jnp.float32,
            )


def products(codes, lefts, rights, sides, finish, out_shape):
    count = len(lefts)
    slots, tile, _ = lefts[0].shape
    halves = len(rights[0])
    right_slots = rights[0][0].shape[0]

    def kernel(codes_ref, *refs):
        left_refs = refs[:count]
        here_refs = refs[count : count + halves]
        there_refs = refs[count + halves : count + 2 * halves]
        outs = refs[count + 2 * halves : -2]
        total_ref, held = refs[-2:]
        row, z, _ = position()
        odd = (row ^ z) & 1
        for m in range(halves):
            held[odd, m] = here_refs[m][...]
            held[1 - odd, m] = there_refs[m][...]
        for side, out_ref in zip(sides, outs):
            total_ref[...] = jnp.zeros_like(total_ref)
            for n, left_ref in enumerate(left_refs):
                at = row ^ odd ^ z ^ (2 * n)
                add_block(
                    codes_ref, n, side, left_ref,
                    lambda found, at=at: held[side >> 1, at + (side & 1), found], right_slots, total_ref,
                )
            finish(total_ref, out_ref)

    return pl.pallas_call(
        kernel,
        out_shape=[out_shape] * len(sides),
        in_specs=[SMEM] + [VMEM] * (count + 2 * halves),
        out_specs=[VMEM] * len(sides),
        scratch_shapes=[
            pltpu.VMEM((RT * tile, tile), jnp.float32),
            pltpu.VMEM((2, halves) + rights[0][0].shape, rights[0][0].dtype),
        ],
        compiler_params=pltpu.CompilerParams(vmem_limit_bytes=32 * 1024 * 1024),
        cost_estimate=pl.CostEstimate(
            flops=2 * len(sides) * count * slots * tile**3,
            bytes_accessed=2 * count * slots * tile**2,
            transcendentals=0,
        ),
    )(codes, *lefts, *rights[0], *rights[1])


def write_sum(sum_ref, out_ref):
    out_ref[...] = sum_ref[...]


def write_coded(sum_ref, out_ref):
    tile = sum_ref.shape[1]
    exponents = jnp.zeros((PAD, tile), jnp.float32)
    for i in range(RT):
        values = sum_ref[i * tile : (i + 1) * tile, :]
        largest = jnp.max(jnp.abs(values), axis=0, keepdims=True)
        exponent = jnp.clip(jnp.floor(jnp.log2(largest)) + 1.0, -LEAST, LEAST)
        coded = jnp.round(values * jnp.exp2(BITS - exponent))
        coded = jnp.clip(coded, -(2.0**BITS) + 1.0, 2.0**BITS - 1.0)
        out_ref[i * tile : (i + 1) * tile, :] = coded.astype(jnp.int32).astype(jnp.int16)
        at = lax.broadcasted_iota(jnp.int32, (PAD, tile), 0)
        exponents = jnp.where(at == i, exponent, exponents)
    out_ref[RT * tile :, :] = exponents.astype(jnp.int32).astype(jnp.int16)


def decoded(coded):
    tile = coded.shape[1]
    exponents = coded[RT * tile : RT * tile + RT].astype(jnp.float32)
    scale = jnp.repeat(jnp.exp2(exponents - BITS), tile, axis=0)
    return coded[: RT * tile].astype(jnp.float32) * scale


def travel(block, source):
    rows, cols = lax.axis_size("row"), lax.axis_size("col")
    route = []
    for r in range(rows):
        for c in range(cols):
            row, z, y = source(r, c >> 1, c & 1)
            route.append((row * cols + 2 * z + y, r * cols + c))
    return lax.ppermute(block, ("row", "col"), route)


def hold(block, flops):
    whole = pl.BlockSpec(memory_space=pl.ANY)
    return pl.pallas_call(
        lambda *refs: None,
        out_shape=jax.ShapeDtypeStruct(block.shape, block.dtype),
        in_specs=[whole],
        out_specs=whole,
        input_output_aliases={0: 0},
        cost_estimate=pl.CostEstimate(flops=flops, bytes_accessed=0, transcendentals=0),
    )(block)


def gather_left(block):
    blocks = {0: block}
    distance = lax.axis_size("col") // 4
    while distance > 1:
        for s in sorted(blocks):
            blocks[s ^ distance] = travel(blocks[s], lambda r, z, y: (r, z ^ distance, y))
        distance //= 2
    return [blocks[s] for s in sorted(blocks)]


def gather_right(right):
    y = lax.axis_index("col") & 1
    given = lax.dynamic_index_in_dim(right, 1 - y, 0, keepdims=False)
    own = lax.dynamic_index_in_dim(right, y, 0, keepdims=False)
    chips = []
    for t in range(0, lax.axis_size("row"), 2):
        for side, half in enumerate((own, given)):

            def source(r, z, y, t=t, side=side):
                odd = (r ^ z) & 1
                return r ^ odd ^ t, z ^ odd, y ^ side

            chips.append(travel(half, source))
    return chips, [travel(half, lambda r, z, y: (r ^ 1, z, y)) for half in chips]


def shards(left_tiles, left_index, right_tiles, right_index):
    codes = find_matches(left_index, right_index)
    own, *lefts = gather_left(left_tiles[0, 0])
    lefts = [own] + [hold(block, FLOPS) for block in lefts]
    rights = gather_right(right_tiles[0, 0])
    tile = left_tiles.shape[-1]
    coded = jax.ShapeDtypeStruct((RT * tile + PAD, tile), jnp.int16)
    plain = jax.ShapeDtypeStruct((RT * tile, tile), jnp.float32)
    to_give = products(codes, lefts, rights, (1, 2, 3), write_coded, coded)
    (total,) = products(codes, lefts, rights, (0,), write_sum, plain)
    for side, block in enumerate(to_give, 1):
        total += decoded(travel(block, lambda r, z, y: (r, z ^ (side >> 1), y ^ (side & 1))))
    return total.astype(jnp.bfloat16)


def solution(mesh):
    return jax.shard_map(
        shards,
        mesh=mesh,
        in_specs=(
            P("row", "col", None, None, None),
            P(),
            P("row", "col", None, None, None, None),
            P(),
        ),
        out_specs=P("row", "col"),
        check_vma=False,
    )
```

profile of v0, /device:TPU:0, one launch (start us, length us, event | category | flops | bytes accessed | tf_op | source)
XLA Modules:
  0.0 28.6 jit_solution(11514017037531571769)
XLA Ops:
  0.0 4.0 %collective-permute-start = (bf16[6,128,128]{2,1,0:T(8,128)(2,1)}, bf16[6,128,128]{2,1,0:T(8,128)(2,1)S(1)}, u32[]{:S(2)}, u32[]{:S(2)}) collective-permute-start(bf16[6,128,128]{2,1,0:T(8,128)(2,1)} %bitcast.25), channel_id=1, source_target_pairs={{4,0},{5,1},{6,2},{7,3},{0,4},{1,5},{2,6},{3,7},{12,8},{13,9},{14,... | collective-permute-start | bytes 589832 | tf_op jit(solution)/shard_map/ppermute | solution.py:152
  4.0 1.0 %dynamic-slice_bitcast_fusion = (bf16[3,128,128]{2,1,0:T(8,128)(2,1)S(1)}, bf16[3,128,128]{2,1,0:T(8,128)(2,1)S(1)}) fusion(bf16[1,1,2,3,128,128]{5,4,3,2,1,0:T(8,128)(2,1)} %param.6, s32[]{:T(128)S(6)} %select_n.8, s32[]{:T(128)S(6)} %select_n.7), kind=kLoop, calls=%fused_computation.7 | loop fusion | bytes 393224 | tf_op jit(solution)/shard_map/jit(dynamic_index_in_dim)/squeeze | solution.py:179
  5.0 2.5 %collective-permute-start.4 = (bf16[3,128,128]{2,1,0:T(8,128)(2,1)S(1)}, bf16[3,128,128]{2,1,0:T(8,128)(2,1)S(1)}, u32[]{:S(2)}, u32[]{:S(2)}) collective-permute-start(bf16[3,128,128]{2,1,0:T(8,128)(2,1)S(1)} %get-tuple-element.11), channel_id=1, source_target_pairs={{17,0},{16,1},{25,2},{24,3},{21,4},{20,5},{29,6},{28,7},{19,8},{18... | collective-permute-start | bytes 294920 | tf_op jit(solution)/shard_map/ppermute | solution.py:152
  7.5 0.5 %collective-permute-start.2 = (bf16[3,128,128]{2,1,0:T(8,128)(2,1)S(1)}, bf16[3,128,128]{2,1,0:T(8,128)(2,1)S(1)}, u32[]{:S(2)}, u32[]{:S(2)}) collective-permute-start(bf16[3,128,128]{2,1,0:T(8,128)(2,1)S(1)} %get-tuple-element.11), channel_id=1, source_target_pairs={{1,0},{0,1},{9,2},{8,3},{5,4},{4,5},{13,6},{12,7},{3,8},{2,9},{11,... | collective-permute-start | bytes 294920 | tf_op jit(solution)/shard_map/ppermute | solution.py:152
  8.0 0.5 %collective-permute-start.3 = (bf16[3,128,128]{2,1,0:T(8,128)(2,1)S(1)}, bf16[3,128,128]{2,1,0:T(8,128)(2,1)S(1)}, u32[]{:S(2)}, u32[]{:S(2)}) collective-permute-start(bf16[3,128,128]{2,1,0:T(8,128)(2,1)S(1)} %get-tuple-element.12), channel_id=1, source_target_pairs={{16,0},{17,1},{24,2},{25,3},{20,4},{21,5},{28,6},{29,7},{18,8},{19... | collective-permute-start | bytes 294920 | tf_op jit(solution)/shard_map/ppermute | solution.py:152
  8.5 0.7 %collective-permute-start.1 = (bf16[3,128,128]{2,1,0:T(8,128)(2,1)S(1)}, bf16[3,128,128]{2,1,0:T(8,128)(2,1)S(1)}, u32[]{:S(2)}, u32[]{:S(2)}) collective-permute-start(bf16[3,128,128]{2,1,0:T(8,128)(2,1)S(1)} %get-tuple-element.12), channel_id=1, source_target_pairs={{0,0},{1,1},{8,2},{9,3},{4,4},{5,5},{12,6},{13,7},{2,8},{3,9},{10,... | collective-permute-start | bytes 294920 | tf_op jit(solution)/shard_map/ppermute | solution.py:152
  9.2 2.0 %shard_map.46.codes_ref = s32[48]{0:T(128)} custom-call(s32[6,4,8]{2,1,0:T(4,128)} %bitcast.28, s32[4,3,2,8]{3,2,1,0:T(2,128)} %bitcast.29), custom_call_target="tpu_custom_call" | custom-call | tf_op jit(solution)/shard_map/pallas_call | solution.py:48
  11.2 0.0 copy-start
  11.2 0.0 copy-start.3
  11.2 0.5 %collective-permute-done.4.refs_5_ = bf16[3,128,128]{2,1,0:T(8,128)(2,1)S(1)} collective-permute-done((bf16[3,128,128]{2,1,0:T(8,128)(2,1)S(1)}, bf16[3,128,128]{2,1,0:T(8,128)(2,1)S(1)}, u32[]{:S(2)}, u32[]{:S(2)}) %collective-permute-start.4) | collective-permute-done | bytes 98336 | tf_op jit(solution)/shard_map/ppermute | solution.py:152
  11.7 2.7 %collective-permute-start.8 = (bf16[3,128,128]{2,1,0:T(8,128)(2,1)S(1)}, bf16[3,128,128]{2,1,0:T(8,128)(2,1)S(1)}, u32[]{:S(2)}, u32[]{:S(2)}) collective-permute-start(bf16[3,128,128]{2,1,0:T(8,128)(2,1)S(1)} %collective-permute-done.4.refs_5_), channel_id=1, source_target_pairs={{8,0},{9,1},{10,2},{11,3},{12,4},{13,5},{14,6},{15,7},{0,8},{1,9},... | collective-permute-start | bytes 294920 | tf_op jit(solution)/shard_map/ppermute | solution.py:152
  14.4 0.0 collective-permute-done.2.refs_3_
  14.4 0.8 %collective-permute-start.6 = (bf16[3,128,128]{2,1,0:T(8,128)(2,1)S(1)}, bf16[3,128,128]{2,1,0:T(8,128)(2,1)S(1)}, u32[]{:S(2)}, u32[]{:S(2)}) collective-permute-start(bf16[3,128,128]{2,1,0:T(8,128)(2,1)S(1)} %collective-permute-done.2.refs_3_), channel_id=1, source_target_pairs={{8,0},{9,1},{10,2},{11,3},{12,4},{13,5},{14,6},{15,7},{0,8},{1,9},... | collective-permute-start | bytes 294920 | tf_op jit(solution)/shard_map/ppermute | solution.py:152
  15.2 0.0 collective-permute-done.3.refs_4_
  15.2 1.0 %collective-permute-start.7 = (bf16[3,128,128]{2,1,0:T(8,128)(2,1)S(1)}, bf16[3,128,128]{2,1,0:T(8,128)(2,1)S(1)}, u32[]{:S(2)}, u32[]{:S(2)}) collective-permute-start(bf16[3,128,128]{2,1,0:T(8,128)(2,1)S(1)} %collective-permute-done.3.refs_4_), channel_id=1, source_target_pairs={{8,0},{9,1},{10,2},{11,3},{12,4},{13,5},{14,6},{15,7},{0,8},{1,9},... | collective-permute-start | bytes 294920 | tf_op jit(solution)/shard_map/ppermute | solution.py:152
  16.3 0.0 collective-permute-done.1.refs_2_
  16.3 0.5 %collective-permute-start.5 = (bf16[3,128,128]{2,1,0:T(8,128)(2,1)S(1)}, bf16[3,128,128]{2,1,0:T(8,128)(2,1)S(1)}, u32[]{:S(2)}, u32[]{:S(2)}) collective-permute-start(bf16[3,128,128]{2,1,0:T(8,128)(2,1)S(1)} %collective-permute-done.1.refs_2_), channel_id=1, source_target_pairs={{8,0},{9,1},{10,2},{11,3},{12,4},{13,5},{14,6},{15,7},{0,8},{1,9},... | collective-permute-start | bytes 294920 | tf_op jit(solution)/shard_map/ppermute | solution.py:152
  16.7 0.0 collective-permute-done.refs_0_
  16.7 0.0 copy-start.1
  16.7 0.7 %copy-done.1 = bf16[6,128,128]{2,1,0:T(8,128)(2,1)} copy-done((bf16[6,128,128]{2,1,0:T(8,128)(2,1)}, bf16[6,128,128]{2,1,0:T(8,128)(2,1)S(1)}, u32[]{:S(2)}) %copy-start.1) | copy-done | bytes 196632
  17.4 0.0 collective-permute-done.8.refs_9_
  17.4 0.0 collective-permute-done.6.refs_7_
  17.4 0.0 collective-permute-done.7.refs_8_
  17.4 0.3 collective-permute-done.5.refs_6_
  17.7 0.0 copy-done
  17.7 0.0 copy-done.3
  17.7 0.0 copy-start.2
  17.7 0.9 %copy-done.2 = bf16[6,128,128]{2,1,0:T(8,128)(2,1)S(1)} copy-done((bf16[6,128,128]{2,1,0:T(8,128)(2,1)S(1)}, bf16[6,128,128]{2,1,0:T(8,128)(2,1)}, u32[]{:S(2)}) %copy-start.2) | copy-done | bytes 196632
  18.6 1.7 %shard_map.49 = (s16[272,128]{1,0:T(8,128)(2,1)S(1)}, s16[272,128]{1,0:T(8,128)(2,1)S(1)}, s16[272,128]{1,0:T(8,128)(2,1)S(1)}) custom-call(s32[48]{0:T(128)S(1)} %copy-done.3, bf16[6,128,128]{2,1,0:T(8,128)(2,1)S(1)} %bitcast.26, bf16[6,128,128]{2,1,0:T(8,128)(2,1)S(1)} %copy-done.2, bf16[3,128,128]{2,1,0:T(8,128)(2,1)S(1)} %collective-permute-done.1.refs_2_, ...), custom_call_target="tpu_custom_call" | custom-call | flops 150994944 | bytes 393216 | tf_op jit(solution)/shard_map/pallas_call | solution.py:101
  20.3 1.2 %collective-permute-start.9 = (s16[272,128]{1,0:T(8,128)(2,1)S(1)}, s16[272,128]{1,0:T(8,128)(2,1)S(1)}, u32[]{:S(2)}, u32[]{:S(2)}) collective-permute-start(s16[272,128]{1,0:T(8,128)(2,1)S(1)} %get-tuple-element.8), channel_id=1, source_target_pairs={{1,0},{0,1},{3,2},{2,3},{5,4},{4,5},{7,6},{6,7},{9,8},{8,9},{11,10... | collective-permute-start | bytes 208904 | tf_op jit(solution)/shard_map/ppermute | solution.py:152
  21.5 0.6 %collective-permute-start.10 = (s16[272,128]{1,0:T(8,128)(2,1)S(1)}, s16[272,128]{1,0:T(8,128)(2,1)S(1)}, u32[]{:S(2)}, u32[]{:S(2)}) collective-permute-start(s16[272,128]{1,0:T(8,128)(2,1)S(1)} %get-tuple-element.9), channel_id=1, source_target_pairs={{2,0},{3,1},{0,2},{1,3},{6,4},{7,5},{4,6},{5,7},{10,8},{11,9},{8,1... | collective-permute-start | bytes 208904 | tf_op jit(solution)/shard_map/ppermute | solution.py:152
  22.1 1.8 %collective-permute-start.11 = (s16[272,128]{1,0:T(8,128)(2,1)S(1)}, s16[272,128]{1,0:T(8,128)(2,1)S(1)}, u32[]{:S(2)}, u32[]{:S(2)}) collective-permute-start(s16[272,128]{1,0:T(8,128)(2,1)S(1)} %get-tuple-element.10), channel_id=1, source_target_pairs={{3,0},{2,1},{1,2},{0,3},{7,4},{6,5},{5,6},{4,7},{11,8},{10,9},{9,1... | collective-permute-start | bytes 208904 | tf_op jit(solution)/shard_map/ppermute | solution.py:152
  23.8 0.9 %shard_map.48 = f32[256,128]{1,0:T(8,128)S(1)} custom-call(s32[48]{0:T(128)S(1)} %copy-done.3, bf16[6,128,128]{2,1,0:T(8,128)(2,1)S(1)} %bitcast.27, bf16[6,128,128]{2,1,0:T(8,128)(2,1)S(1)} %copy-done.2, bf16[3,128,128]{2,1,0:T(8,128)(2,1)S(1)} %collective-permute-done.1.refs_2_, bf16[3,128,128]{2,1,0:T(8,128)(2,1)S(1)} %collective-permute-done.2.refs_3_, ...), custom_call_target="tpu_custom_call" | custom-call | flops 50331648 | bytes 393216 | tf_op jit(solution)/shard_map/pallas_call | solution.py:101
  24.8 0.4 %collective-permute-done.9 = s16[272,128]{1,0:T(8,128)(2,1)S(1)} collective-permute-done((s16[272,128]{1,0:T(8,128)(2,1)S(1)}, s16[272,128]{1,0:T(8,128)(2,1)S(1)}, u32[]{:S(2)}, u32[]{:S(2)}) %collective-permute-start.9) | collective-permute-done | bytes 69664 | tf_op jit(solution)/shard_map/ppermute | solution.py:152
  25.2 1.2 %collective-permute-done.10 = s16[272,128]{1,0:T(8,128)(2,1)S(1)} collective-permute-done((s16[272,128]{1,0:T(8,128)(2,1)S(1)}, s16[272,128]{1,0:T(8,128)(2,1)S(1)}, u32[]{:S(2)}, u32[]{:S(2)}) %collective-permute-start.10) | collective-permute-done | bytes 69664 | tf_op jit(solution)/shard_map/ppermute | solution.py:152
  26.4 1.5 %collective-permute-done.11 = s16[272,128]{1,0:T(8,128)(2,1)S(1)} collective-permute-done((s16[272,128]{1,0:T(8,128)(2,1)S(1)}, s16[272,128]{1,0:T(8,128)(2,1)S(1)}, u32[]{:S(2)}, u32[]{:S(2)}) %collective-permute-start.11) | collective-permute-done | bytes 69664 | tf_op jit(solution)/shard_map/ppermute | solution.py:152
  27.9 0.7 %fusion.1 = bf16[256,128]{1,0:T(8,128)(2,1)} fusion(f32[256,128]{1,0:T(8,128)S(1)} %shard_map.48, s16[272,128]{1,0:T(8,128)(2,1)S(1)} %collective-permute-done.11, s16[272,128]{1,0:T(8,128)(2,1)S(1)} %collective-permute-done.10, s16[272,128]{1,0:T(8,128)(2,1)S(1)} %collective-permute-done.9, f32[2,128]{1,0:T(2,128)S(1)} %multiply_exponential_fusion, ...), kind=kLoop, calls=%fused_computation.2 | loop fusion | flops 327680 | bytes 396288 | tf_op jit(solution)/shard_map/convert_element_type | solution.py:205
  (4 shorter events, 0.0 us)
Async XLA Ops:
  0.0 16.7 %collective-permute-start = (bf16[6,128,128]{2,1,0:T(8,128)(2,1)}, bf16[6,128,128]{2,1,0:T(8,128)(2,1)S(1)}, u32[]{:S(2)}, u32[]{:S(2)}) collective-permute-start(bf16[6,128,128]{2,1,0:T(8,128)(2,1)} %bitcast.25), channel_id=1, source_target_pairs={{4,0},{5,1},{6,2},{7,3},{0,4},{1,5},{2,6},{3,7},{12,8},{13,9},{14,... | collective-permute-start | bytes 589832 | tf_op jit(solution)/shard_map/ppermute | solution.py:152
  5.0 6.7 %collective-permute-start.4 = (bf16[3,128,128]{2,1,0:T(8,128)(2,1)S(1)}, bf16[3,128,128]{2,1,0:T(8,128)(2,1)S(1)}, u32[]{:S(2)}, u32[]{:S(2)}) collective-permute-start(bf16[3,128,128]{2,1,0:T(8,128)(2,1)S(1)} %get-tuple-element.11), channel_id=1, source_target_pairs={{17,0},{16,1},{25,2},{24,3},{21,4},{20,5},{29,6},{28,7},{19,8},{18... | collective-permute-start | bytes 294920 | tf_op jit(solution)/shard_map/ppermute | solution.py:152
  7.5 6.9 %collective-permute-start.2 = (bf16[3,128,128]{2,1,0:T(8,128)(2,1)S(1)}, bf16[3,128,128]{2,1,0:T(8,128)(2,1)S(1)}, u32[]{:S(2)}, u32[]{:S(2)}) collective-permute-start(bf16[3,128,128]{2,1,0:T(8,128)(2,1)S(1)} %get-tuple-element.11), channel_id=1, source_target_pairs={{1,0},{0,1},{9,2},{8,3},{5,4},{4,5},{13,6},{12,7},{3,8},{2,9},{11,... | collective-permute-start | bytes 294920 | tf_op jit(solution)/shard_map/ppermute | solution.py:152
  8.0 7.2 %collective-permute-start.3 = (bf16[3,128,128]{2,1,0:T(8,128)(2,1)S(1)}, bf16[3,128,128]{2,1,0:T(8,128)(2,1)S(1)}, u32[]{:S(2)}, u32[]{:S(2)}) collective-permute-start(bf16[3,128,128]{2,1,0:T(8,128)(2,1)S(1)} %get-tuple-element.12), channel_id=1, source_target_pairs={{16,0},{17,1},{24,2},{25,3},{20,4},{21,5},{28,6},{29,7},{18,8},{19... | collective-permute-start | bytes 294920 | tf_op jit(solution)/shard_map/ppermute | solution.py:152
  8.5 7.7 %collective-permute-start.1 = (bf16[3,128,128]{2,1,0:T(8,128)(2,1)S(1)}, bf16[3,128,128]{2,1,0:T(8,128)(2,1)S(1)}, u32[]{:S(2)}, u32[]{:S(2)}) collective-permute-start(bf16[3,128,128]{2,1,0:T(8,128)(2,1)S(1)} %get-tuple-element.12), channel_id=1, source_target_pairs={{0,0},{1,1},{8,2},{9,3},{4,4},{5,5},{12,6},{13,7},{2,8},{3,9},{10,... | collective-permute-start | bytes 294920 | tf_op jit(solution)/shard_map/ppermute | solution.py:152
  11.2 6.5 %copy-start = (bf16[1,1,6,128,128]{4,3,2,1,0:T(8,128)(2,1)S(1)}, bf16[1,1,6,128,128]{4,3,2,1,0:T(8,128)(2,1)}, u32[]{:S(2)}) copy-start(bf16[1,1,6,128,128]{4,3,2,1,0:T(8,128)(2,1)} %param.4) | copy-start | bytes 589828
  11.2 6.5 %copy-start.3 = (s32[48]{0:T(128)S(1)}, s32[48]{0:T(128)}, u32[]{:S(2)}) copy-start(s32[48]{0:T(128)} %shard_map.46.codes_ref) | copy-start | bytes 580
  11.7 5.7 %collective-permute-start.8 = (bf16[3,128,128]{2,1,0:T(8,128)(2,1)S(1)}, bf16[3,128,128]{2,1,0:T(8,128)(2,1)S(1)}, u32[]{:S(2)}, u32[]{:S(2)}) collective-permute-start(bf16[3,128,128]{2,1,0:T(8,128)(2,1)S(1)} %collective-permute-done.4.refs_5_), channel_id=1, source_target_pairs={{8,0},{9,1},{10,2},{11,3},{12,4},{13,5},{14,6},{15,7},{0,8},{1,9},... | collective-permute-start | bytes 294920 | tf_op jit(solution)/shard_map/ppermute | solution.py:152
  14.4 3.0 %collective-permute-start.6 = (bf16[3,128,128]{2,1,0:T(8,128)(2,1)S(1)}, bf16[3,128,128]{2,1,0:T(8,128)(2,1)S(1)}, u32[]{:S(2)}, u32[]{:S(2)}) collective-permute-start(bf16[3,128,128]{2,1,0:T(8,128)(2,1)S(1)} %collective-permute-done.2.refs_3_), channel_id=1, source_target_pairs={{8,0},{9,1},{10,2},{11,3},{12,4},{13,5},{14,6},{15,7},{0,8},{1,9},... | collective-permute-start | bytes 294920 | tf_op jit(solution)/shard_map/ppermute | solution.py:152
  15.2 2.2 %collective-permute-start.7 = (bf16[3,128,128]{2,1,0:T(8,128)(2,1)S(1)}, bf16[3,128,128]{2,1,0:T(8,128)(2,1)S(1)}, u32[]{:S(2)}, u32[]{:S(2)}) collective-permute-start(bf16[3,128,128]{2,1,0:T(8,128)(2,1)S(1)} %collective-permute-done.3.refs_4_), channel_id=1, source_target_pairs={{8,0},{9,1},{10,2},{11,3},{12,4},{13,5},{14,6},{15,7},{0,8},{1,9},... | collective-permute-start | bytes 294920 | tf_op jit(solution)/shard_map/ppermute | solution.py:152
  16.3 1.4 %collective-permute-start.5 = (bf16[3,128,128]{2,1,0:T(8,128)(2,1)S(1)}, bf16[3,128,128]{2,1,0:T(8,128)(2,1)S(1)}, u32[]{:S(2)}, u32[]{:S(2)}) collective-permute-start(bf16[3,128,128]{2,1,0:T(8,128)(2,1)S(1)} %collective-permute-done.1.refs_2_), channel_id=1, source_target_pairs={{8,0},{9,1},{10,2},{11,3},{12,4},{13,5},{14,6},{15,7},{0,8},{1,9},... | collective-permute-start | bytes 294920 | tf_op jit(solution)/shard_map/ppermute | solution.py:152
  16.7 0.7 %copy-start.1 = (bf16[6,128,128]{2,1,0:T(8,128)(2,1)}, bf16[6,128,128]{2,1,0:T(8,128)(2,1)S(1)}, u32[]{:S(2)}) copy-start(bf16[6,128,128]{2,1,0:T(8,128)(2,1)S(1)} %collective-permute-done.refs_0_) | copy-start | bytes 589828
  17.7 0.9 %copy-start.2 = (bf16[6,128,128]{2,1,0:T(8,128)(2,1)S(1)}, bf16[6,128,128]{2,1,0:T(8,128)(2,1)}, u32[]{:S(2)}) copy-start(bf16[6,128,128]{2,1,0:T(8,128)(2,1)} %shard_map.47.refs_1_) | copy-start | bytes 589828
  20.3 4.9 %collective-permute-start.9 = (s16[272,128]{1,0:T(8,128)(2,1)S(1)}, s16[272,128]{1,0:T(8,128)(2,1)S(1)}, u32[]{:S(2)}, u32[]{:S(2)}) collective-permute-start(s16[272,128]{1,0:T(8,128)(2,1)S(1)} %get-tuple-element.8), channel_id=1, source_target_pairs={{1,0},{0,1},{3,2},{2,3},{5,4},{4,5},{7,6},{6,7},{9,8},{8,9},{11,10... | collective-permute-start | bytes 208904 | tf_op jit(solution)/shard_map/ppermute | solution.py:152
  21.5 4.9 %collective-permute-start.10 = (s16[272,128]{1,0:T(8,128)(2,1)S(1)}, s16[272,128]{1,0:T(8,128)(2,1)S(1)}, u32[]{:S(2)}, u32[]{:S(2)}) collective-permute-start(s16[272,128]{1,0:T(8,128)(2,1)S(1)} %get-tuple-element.9), channel_id=1, source_target_pairs={{2,0},{3,1},{0,2},{1,3},{6,4},{7,5},{4,6},{5,7},{10,8},{11,9},{8,1... | collective-permute-start | bytes 208904 | tf_op jit(solution)/shard_map/ppermute | solution.py:152
  22.1 5.8 %collective-permute-start.11 = (s16[272,128]{1,0:T(8,128)(2,1)S(1)}, s16[272,128]{1,0:T(8,128)(2,1)S(1)}, u32[]{:S(2)}, u32[]{:S(2)}) collective-permute-start(s16[272,128]{1,0:T(8,128)(2,1)S(1)} %get-tuple-element.10), channel_id=1, source_target_pairs={{3,0},{2,1},{1,2},{0,3},{7,4},{6,5},{5,6},{4,7},{11,8},{10,9},{9,1... | collective-permute-start | bytes 208904 | tf_op jit(solution)/shard_map/ppermute | solution.py:152
where the time goes:
time: 28.8 us; the launch traced here: 28.6 us
  starting transfers between devices  16.8 us (58%)
  Pallas kernels  4.54 us (16%)
  waiting for transfers between devices  3.81 us (13%)
  local copies, waits for them, and re-layouts  2.56 us (9%)
  other arithmetic  0.75 us (3%)
    ppermute x12, starting transfers between devices, travel(): return lax.ppermute(block, ('row', 'col'), route)  16.8 us
    ppermute x12, waiting for transfers between devices, travel(): return lax.ppermute(block, ('row', 'col'), route)  3.81 us
    pallas_call x2, Pallas kernels, products(): pl.pallas_call(kernel, out_shape=[out_shape] * len(sides), in_specs=[SMEM...  2.58 us
    pallas_call x1, Pallas kernels, find_matches(): pl.pallas_call(kernel, out_shape=jax.ShapeDtypeStruct((inner // 2 * SIDES...  1.96 us
    unnamed x8, local copies, waits for them, and re-layouts  1.61 us
    squeeze x1, local copies, waits for them, and re-layouts, gather_right(): given = lax.dynamic_index_in_dim(right, 1 - y, 0, keepdims=False)  0.95 us
    convert_element_type x1, other arithmetic, shards(): return total.astype(jnp.bfloat16)  0.72 us
  transfers between devices with their start and end apart: 12, of which 5 were waited for; matrix products, arithmetic and copies ran while one was open for 3% of the time, Pallas kernels for 10%

commit v1 on v0

v1 whole, which is shorter than its diff:
```python
import jax
import jax.numpy as jnp
from jax import lax
from jax.experimental import pallas as pl
from jax.experimental.pallas import tpu as pltpu
from jax.sharding import PartitionSpec as P

KT = 8
RT = 2
SIDES = 3
EARLY = 10**8
LATE = 10**11
BITS = 15
LEAST = 100
PAD = 16
SMEM = pl.BlockSpec(memory_space=pltpu.SMEM)
VMEM = pl.BlockSpec(memory_space=pltpu.VMEM)


def position():
    col = lax.axis_index("col")
    return lax.axis_index("row"), col >> 1, col & 1


def counting(side, places):
    early = [s for s in range(places) if s % 2 == 0 or s == 1]
    return [range(places), early, [s for s in early if s > 1]][side]


def code_at(s, side, places, slots):
    pairs = [(other, at) for at in range(SIDES) for other in counting(at, places)]
    return pairs.index((s, side)) * slots


def find_matches(left_index, right_index):
    slots = left_index.shape[-1]
    places, _, _, right_slots = right_index.shape
    left_index = left_index.transpose(2, 0, 1)
    right_index = right_index.transpose(0, 3, 2, 1)
    total = sum(len(counting(side, places)) for side in range(SIDES)) * slots

    def kernel(li_ref, ri_ref, codes_ref):
        row, z, y = position()
        for side in range(SIDES):
            column = 2 * (z ^ (side >> 1)) + (y ^ min(side, 1))
            for s in counting(side, places):
                zp = z ^ s
                base = code_at(s, side, places, slots)
                have = [ri_ref[zp, t, y, column] for t in range(right_slots)]

                @pl.loop(0, slots)
                def _(slot):
                    at = li_ref[slot, row, 2 * zp + y]
                    k = lax.rem(at, KT)
                    first = 1 + lax.div(at, KT) * right_slots
                    code = jnp.int32(0)
                    for t in range(right_slots):
                        code = jnp.where(have[t] == k, first + t, code)
                    codes_ref[base + slot] = jnp.where(at < RT * KT, code, 0)

    return pl.pallas_call(
        kernel,
        out_shape=jax.ShapeDtypeStruct((total,), jnp.int32),
        in_specs=[SMEM] * 2,
        out_specs=SMEM,
    )(left_index, right_index)


def add_block(codes_ref, base, left_ref, right_at, right_slots, total_ref):
    slots, tile, _ = left_ref.shape

    @pl.loop(0, slots)
    def _(slot):
        code = codes_ref[base + slot]

        @pl.when(code > 0)
        def _():
            i = lax.div(code - 1, right_slots)
            rows = pl.ds(pl.multiple_of(i * tile, tile), tile)
            total_ref[rows, :] += jnp.dot(
                left_ref[slot],
                right_at(lax.rem(code - 1, right_slots)),
                preferred_element_type=jnp.float32,
            )


def products(codes, lefts, rights, sides, finish, out_shape, flops, start=None):
    distances = sorted(lefts)
    count = len(lefts)
    places = len(rights) // 2
    right_slots, tile, _ = rights[0].shape
    slots = lefts[distances[0]].shape[0]
    starts = [] if start is None else [start]

    def kernel(codes_ref, *refs):
        left_refs = dict(zip(distances, refs))
        right_refs = refs[count : count + 2 * places]
        start_refs = refs[count + 2 * places :][: len(starts)]
        outs = refs[count + 2 * places + len(starts) : -2]
        total_ref, held = refs[-2:]
        row, z, _ = position()
        for at in sorted({min(side, 1) for side in sides}):
            for t in range(places):
                held[t, at] = right_refs[2 * t + at][...]
        for side, out_ref in zip(sides, outs):
            total_ref[...] = start_refs[0][...] if starts else jnp.zeros_like(total_ref)
            for s in counting(side, places):
                if s in left_refs:
                    t = row ^ z ^ s ^ (side >> 1)
                    add_block(
                        codes_ref, code_at(s, side, places, slots), left_refs[s],
                        lambda found, t=t: held[t, min(side, 1), found], right_slots, total_ref,
                    )
            finish(total_ref, out_ref)

    return pl.pallas_call(
        kernel,
        out_shape=[out_shape] * len(sides),
        in_specs=[SMEM] + [VMEM] * (count + 2 * places + len(starts)),
        out_specs=[VMEM] * len(sides),
        scratch_shapes=[
            pltpu.VMEM((RT * tile, tile), jnp.float32),
            pltpu.VMEM((places, 2, right_slots, tile, tile), jnp.bfloat16),
        ],
        compiler_params=pltpu.CompilerParams(vmem_limit_bytes=32 * 1024 * 1024),
        cost_estimate=pl.CostEstimate(
            flops=flops,
            bytes_accessed=2 * count * slots * tile**2,
            transcendentals=0,
        ),
    )(codes, *[lefts[s] for s in distances], *rights, *starts)


def write_sum(sum_ref, out_ref):
    out_ref[...] = sum_ref[...]


def write_coded(sum_ref, out_ref):
    tile = sum_ref.shape[1]
    exponents = jnp.zeros((PAD, tile), jnp.float32)
    for i in range(RT):
        values = sum_ref[i * tile : (i + 1) * tile, :]
        largest = jnp.max(jnp.abs(values), axis=0, keepdims=True)
        exponent = jnp.clip(jnp.floor(jnp.log2(largest)) + 1.0, -LEAST, LEAST)
        coded = jnp.round(values * jnp.exp2(BITS - exponent))
        coded = jnp.clip(coded, -(2.0**BITS) + 1.0, 2.0**BITS - 1.0)
        out_ref[i * tile : (i + 1) * tile, :] = coded.astype(jnp.int32).astype(jnp.int16)
        at = lax.broadcasted_iota(jnp.int32, (PAD, tile), 0)
        exponents = jnp.where(at == i, exponent, exponents)
    out_ref[RT * tile :, :] = exponents.astype(jnp.int32).astype(jnp.int16)


def decoded(coded):
    tile = coded.shape[1]
    exponents = coded[RT * tile : RT * tile + RT].astype(jnp.float32)
    scale = jnp.repeat(jnp.exp2(exponents - BITS), tile, axis=0)
    return coded[: RT * tile].astype(jnp.float32) * scale


def across(block, axis, mask):
    route = [(i, i ^ mask) for i in range(lax.axis_size(axis))]
    return lax.ppermute(block, axis, route)


def travel(block, source):
    rows, cols = lax.axis_size("row"), lax.axis_size("col")
    route = []
    for r in range(rows):
        for c in range(cols):
            row, z, y = source(r, c >> 1, c & 1)
            route.append((row * cols + 2 * z + y, r * cols + c))
    return lax.ppermute(block, ("row", "col"), route)


def other_half(given, t):
    def source(r, z, y):
        apart = r ^ t ^ z
        swap = apart % 2 if apart > 1 else 0
        return r ^ t ^ swap, z ^ swap, y ^ 1

    return travel(given, source)


def gather(block, beside, ahead):
    distance = lax.axis_size("col") // 4
    steps = [distance >> n for n in range(distance.bit_length())]
    later, ahead = lax.optimization_barrier((block, ahead))
    came = [across(later if d == 1 else block, "col", 2 * d) for d in steps]
    came[:-1], beside = lax.optimization_barrier((came[:-1], beside))
    blocks = {0: block, **dict(zip(steps, came))}
    for d in steps:
        for s in sorted(blocks):
            if s ^ d not in blocks and s & (d - 1) == 0:
                blocks[s ^ d] = across(blocks[s], "col", 2 * d)
    return blocks, beside, ahead


def shards(left_tiles, left_index, right_tiles, right_index):
    y = lax.axis_index("col") & 1
    left = left_tiles[0, 0]
    right = right_tiles[0, 0]
    tile = left.shape[-1]

    codes = find_matches(left_index, right_index)
    given = lax.dynamic_index_in_dim(right, 1 - y, 0, keepdims=False)
    own = lax.dynamic_index_in_dim(right, y, 0, keepdims=False)
    lefts, codes, (own, given) = gather(left, codes, (own, given))
    rights = []
    for t in range(0, lax.axis_size("row"), 2):
        pair = [across(own, "row", t) if t else own, other_half(given, t)]
        if not t:
            pair[0], lefts[1] = lax.optimization_barrier((pair[0], lefts[1]))
        rights += pair + [across(half, "row", 1) for half in pair]

    plain = jax.ShapeDtypeStruct((RT * tile, tile), jnp.float32)
    coded = jax.ShapeDtypeStruct((RT * tile + PAD, tile), jnp.int16)
    early = {s: lefts[s] for s in counting(1, len(lefts))}
    late = {s: lefts[s] for s in lefts if s not in early}
    to_other, to_far = products(codes, early, rights, (1, 2), write_coded, coded, EARLY)
    coming = across(to_other, "col", 1)
    from_far = across(to_far, "col", 3)
    (mine,) = products(codes, early, rights, (0,), write_sum, plain, 10**8)
    (mine,) = products(codes, late, rights, (0,), write_sum, plain, LATE, mine)
    mine, coming, from_far = lax.optimization_barrier((mine, coming, from_far))
    return (mine + decoded(coming) + decoded(from_far)).astype(jnp.bfloat16)


def solution(mesh):
    return jax.shard_map(
        shards,
        mesh=mesh,
        in_specs=(
            P("row", "col", None, None, None),
            P(),
            P("row", "col", None, None, None, None),
            P(),
        ),
        out_specs=P("row", "col"),
        check_vma=False,
    )
```

time: 28.8 us -> 28.3 us (0.983)
  Pallas kernels: 4.54 us -> 5.48 us
  local copies, waits for them, and re-layouts: 2.56 us -> 1.67 us
  starting transfers between devices: 16.8 us -> 16.3 us
    ppermute x12 -> x2, starting transfers between devices: 16.8 us -> 2 us  [travel(): return lax.ppermute(block, ('row', 'col'), route)]
    ppermute x0 -> x10, starting transfers between devices: none -> 14.3 us  [across(): return lax.ppermute(block, axis, route)]
    ppermute x12 -> x2, waiting for transfers between devices: 3.81 us -> 0.01 us  [travel(): return lax.ppermute(block, ('row', 'col'), route)]
    ppermute x0 -> x10, waiting for transfers between devices: none -> 3.75 us  [across(): return lax.ppermute(block, axis, route)]
    unnamed x8 -> x4, local copies, waits for them, and re-layouts: 1.61 us -> 0.68 us
    pallas_call x2 -> x3, Pallas kernels: 2.58 us -> 3.18 us  [products(): pl.pallas_call(kernel, out_shape=[out_shape] * len(sides), in_specs=[SMEM...]
    pallas_call x2 -> x1, Pallas kernels: 1.96 us -> 2.3 us  [find_matches(): pl.pallas_call(kernel, out_shape=jax.ShapeDtypeStruct((total,), jnp.int32...]
  transfers between devices with their start and end apart: 12 -> 12, of which waited for: 5 -> 5; matrix products, arithmetic and copies ran while one was open for 3% -> 4% of each run, Pallas kernels for 10% -> 20%
where the time goes in v1:
time: 28.3 us; the launch traced here: 28 us
  starting transfers between devices  16.3 us (58%)
  Pallas kernels  5.48 us (19%)
  waiting for transfers between devices  3.75 us (13%)
  local copies, waits for them, and re-layouts  1.67 us (6%)
  other arithmetic  0.7 us (2%)
    ppermute x10, starting transfers between devices, across(): return lax.ppermute(block, axis, route)  14.3 us
    ppermute x10, waiting for transfers between devices, across(): return lax.ppermute(block, axis, route)  3.75 us
    pallas_call x3, Pallas kernels, products(): pl.pallas_call(kernel, out_shape=[out_shape] * len(sides), in_specs=[SMEM...  3.18 us
    pallas_call x1, Pallas kernels, find_matches(): pl.pallas_call(kernel, out_shape=jax.ShapeDtypeStruct((total,), jnp.int32...  2.3 us
    ppermute x2, starting transfers between devices, travel(): return lax.ppermute(block, ('row', 'col'), route)  2 us
    squeeze x1, local copies, waits for them, and re-layouts, shards(): given = lax.dynamic_index_in_dim(right, 1 - y, 0, keepdims=False)  0.99 us
    convert_element_type x1, other arithmetic, shards(): return (mine + decoded(coming) + decoded(from_far)).astype(jnp.bfloat16)  0.69 us
    unnamed x4, local copies, waits for them, and re-layouts  0.68 us
  transfers between devices with their start and end apart: 12, of which 5 were waited for; matrix products, arithmetic and copies ran while one was open for 4% of the time, Pallas kernels for 20%

profile of v1, /device:TPU:0, one launch (start us, length us, event | category | flops | bytes accessed | tf_op | source)
XLA Modules:
  0.0 28.0 jit_solution(6416318179194381438)
XLA Ops:
  0.0 4.0 %collective-permute-start = (bf16[6,128,128]{2,1,0:T(8,128)(2,1)}, bf16[6,128,128]{2,1,0:T(8,128)(2,1)S(1)}, u32[]{:S(2)}, u32[]{:S(2)}) collective-permute-start(bf16[6,128,128]{2,1,0:T(8,128)(2,1)} %bitcast.19), channel_id=1, source_target_pairs={{0,4},{1,5},{2,6},{3,7},{4,0},{5,1},{6,2},{7,3},{8,12},{9,13},{10,... | collective-permute-start | bytes 589832 | tf_op jit(solution)/shard_map/ppermute | solution.py:162
  4.0 0.0 copy-start
  4.0 1.0 %dynamic-slice_bitcast_fusion = (bf16[3,128,128]{2,1,0:T(8,128)(2,1)S(1)}, bf16[3,128,128]{2,1,0:T(8,128)(2,1)S(1)}) fusion(bf16[1,1,2,3,128,128]{5,4,3,2,1,0:T(8,128)(2,1)} %param.6, s32[]{:T(128)S(6)} %select_n.8, s32[]{:T(128)S(6)} %select_n.7), kind=kLoop, calls=%fused_computation.5 | loop fusion | bytes 393224 | tf_op jit(solution)/shard_map/jit(dynamic_index_in_dim)/squeeze | solution.py:205
  5.0 0.0 copy-done
  5.1 1.6 %collective-permute-start.2 = (bf16[6,128,128]{2,1,0:T(8,128)(2,1)S(1)}, bf16[6,128,128]{2,1,0:T(8,128)(2,1)S(1)}, u32[]{:S(2)}, u32[]{:S(2)}) collective-permute-start(bf16[6,128,128]{2,1,0:T(8,128)(2,1)S(1)} %bitcast.20), channel_id=1, source_target_pairs={{0,2},{1,3},{2,0},{3,1},{4,6},{5,7},{6,4},{7,5},{8,10},{9,11},{10,... | collective-permute-start | bytes 589832 | tf_op jit(solution)/shard_map/ppermute | solution.py:162
  6.7 1.5 %collective-permute-start.6 = (bf16[3,128,128]{2,1,0:T(8,128)(2,1)S(1)}, bf16[3,128,128]{2,1,0:T(8,128)(2,1)S(1)}, u32[]{:S(2)}, u32[]{:S(2)}) collective-permute-start(bf16[3,128,128]{2,1,0:T(8,128)(2,1)S(1)} %get-tuple-element.21.refs_3_.refs_1_), channel_id=1, source_target_pairs={{0,16},{8,24},{16,0},{24,8},{1,17},{9,25},{17,1},{25,9},{2,18},{10... | collective-permute-start | bytes 294920 | tf_op jit(solution)/shard_map/ppermute | solution.py:162
  8.2 1.5 %collective-permute-start.7 = (bf16[3,128,128]{2,1,0:T(8,128)(2,1)S(1)}, bf16[3,128,128]{2,1,0:T(8,128)(2,1)S(1)}, u32[]{:S(2)}, u32[]{:S(2)}) collective-permute-start(bf16[3,128,128]{2,1,0:T(8,128)(2,1)S(1)} %get-tuple-element.22), channel_id=1, source_target_pairs={{17,0},{16,1},{25,2},{24,3},{21,4},{20,5},{23,6},{22,7},{19,8},{18... | collective-permute-start | bytes 294920 | tf_op jit(solution)/shard_map/ppermute | solution.py:172
  9.7 0.5 %collective-permute-start.3 = (bf16[3,128,128]{2,1,0:T(8,128)(2,1)S(1)}, bf16[3,128,128]{2,1,0:T(8,128)(2,1)S(1)}, u32[]{:S(2)}, u32[]{:S(2)}) collective-permute-start(bf16[3,128,128]{2,1,0:T(8,128)(2,1)S(1)} %get-tuple-element.22), channel_id=1, source_target_pairs={{1,0},{0,1},{3,2},{2,3},{5,4},{4,5},{13,6},{12,7},{9,8},{8,9},{11,... | collective-permute-start | bytes 294920 | tf_op jit(solution)/shard_map/ppermute | solution.py:172
  10.2 2.3 %shard_map.46.codes_ref = s32[48]{0:T(128)} custom-call(s32[6,4,8]{2,1,0:T(4,128)} %bitcast.23, s32[4,3,2,8]{3,2,1,0:T(2,128)} %bitcast.24), custom_call_target="tpu_custom_call" | custom-call | tf_op jit(solution)/shard_map/pallas_call | solution.py:61
  12.5 1.0 %collective-permute-done.refs_2_ = bf16[6,128,128]{2,1,0:T(8,128)(2,1)S(1)} collective-permute-done((bf16[6,128,128]{2,1,0:T(8,128)(2,1)}, bf16[6,128,128]{2,1,0:T(8,128)(2,1)S(1)}, u32[]{:S(2)}, u32[]{:S(2)}) %collective-permute-start) | collective-permute-done | bytes 196640 | tf_op jit(solution)/shard_map/ppermute | solution.py:162
  13.5 0.8 %collective-permute-start.1 = (bf16[6,128,128]{2,1,0:T(8,128)(2,1)S(1)}, bf16[6,128,128]{2,1,0:T(8,128)(2,1)S(1)}, u32[]{:S(2)}, u32[]{:S(2)}) collective-permute-start(bf16[6,128,128]{2,1,0:T(8,128)(2,1)S(1)} %collective-permute-done.refs_2_), channel_id=1, source_target_pairs={{0,2},{1,3},{2,0},{3,1},{4,6},{5,7},{6,4},{7,5},{8,10},{9,11},{10,... | collective-permute-start | bytes 589832 | tf_op jit(solution)/shard_map/ppermute | solution.py:162
  14.2 0.0 collective-permute-done.6.refs_7_.refs_5_
  14.2 0.0 collective-permute-start.8
  14.2 0.0 collective-permute-done.7.refs_8_.refs_6_
  14.2 3.5 %collective-permute-start.9 = (bf16[3,128,128]{2,1,0:T(8,128)(2,1)S(1)}, bf16[3,128,128]{2,1,0:T(8,128)(2,1)S(1)}, u32[]{:S(2)}, u32[]{:S(2)}) collective-permute-start(bf16[3,128,128]{2,1,0:T(8,128)(2,1)S(1)} %collective-permute-done.7.refs_8_.refs_6_), channel_id=1, source_target_pairs={{0,8},{8,0},{16,24},{24,16},{1,9},{9,1},{17,25},{25,17},{2,10},{10... | collective-permute-start | bytes 294920 | tf_op jit(solution)/shard_map/ppermute | solution.py:162
  17.8 0.0 collective-permute-done.3.refs_4_.refs_2_
  17.8 0.0 collective-permute-start.5
  17.8 0.0 collective-permute-done.2.refs_1_
  17.8 0.5 %collective-permute-start.4 = (bf16[3,128,128]{2,1,0:T(8,128)(2,1)S(1)}, bf16[3,128,128]{2,1,0:T(8,128)(2,1)S(1)}, u32[]{:S(2)}, u32[]{:S(2)}) collective-permute-start(bf16[3,128,128]{2,1,0:T(8,128)(2,1)S(1)} %get-tuple-element.21.refs_3_.refs_1_), channel_id=1, source_target_pairs={{0,8},{8,0},{16,24},{24,16},{1,9},{9,1},{17,25},{25,17},{2,10},{10... | collective-permute-start | bytes 294920 | tf_op jit(solution)/shard_map/ppermute | solution.py:162
  18.3 0.0 collective-permute-done.8.refs_9_.refs_7_
  18.3 0.4 %collective-permute-done.9.refs_10_.refs_8_ = bf16[3,128,128]{2,1,0:T(8,128)(2,1)S(1)} collective-permute-done((bf16[3,128,128]{2,1,0:T(8,128)(2,1)S(1)}, bf16[3,128,128]{2,1,0:T(8,128)(2,1)S(1)}, u32[]{:S(2)}, u32[]{:S(2)}) %collective-permute-start.9) | collective-permute-done | bytes 98336 | tf_op jit(solution)/shard_map/ppermute | solution.py:162
  18.7 0.4 %collective-permute-done.5.refs_6_.refs_4_ = bf16[3,128,128]{2,1,0:T(8,128)(2,1)S(1)} collective-permute-done((bf16[3,128,128]{2,1,0:T(8,128)(2,1)S(1)}, bf16[3,128,128]{2,1,0:T(8,128)(2,1)S(1)}, u32[]{:S(2)}, u32[]{:S(2)}) %collective-permute-start.5) | collective-permute-done | bytes 98336 | tf_op jit(solution)/shard_map/ppermute | solution.py:162
  19.1 0.2 collective-permute-done.4.refs_5_.refs_3_
  19.2 0.0 copy-start.1
  19.2 0.7 %copy-done.1 = s32[48]{0:T(128)S(1)} copy-done((s32[48]{0:T(128)S(1)}, s32[48]{0:T(128)}, u32[]{:S(2)}) %copy-start.1) | copy-done | bytes 216
  19.9 1.5 %shard_map.49 = (s16[272,128]{1,0:T(8,128)(2,1)S(1)}, s16[272,128]{1,0:T(8,128)(2,1)S(1)}) custom-call(s32[48]{0:T(128)S(1)} %copy-done.1, bf16[6,128,128]{2,1,0:T(8,128)(2,1)S(1)} %bitcast.21, bf16[6,128,128]{2,1,0:T(8,128)(2,1)S(1)} %collective-permute-done.2.refs_1_, bf16[6,128,128]{2,1,0:T(8,128)(2,1)S(1)} %collective-permute-done.refs_2_, ...), custom_call_target="tpu_custom_call" | custom-call | flops 100000000 | bytes 589824 | tf_op jit(solution)/shard_map/pallas_call | solution.py:116
  21.4 0.6 %collective-permute-start.10 = (s16[272,128]{1,0:T(8,128)(2,1)S(1)}, s16[272,128]{1,0:T(8,128)(2,1)S(1)}, u32[]{:S(2)}, u32[]{:S(2)}) collective-permute-start(s16[272,128]{1,0:T(8,128)(2,1)S(1)} %get-tuple-element.24), channel_id=1, source_target_pairs={{0,1},{1,0},{2,3},{3,2},{4,5},{5,4},{6,7},{7,6},{8,9},{9,8},{10,11... | collective-permute-start | bytes 208904 | tf_op jit(solution)/shard_map/ppermute | solution.py:162
  22.0 1.7 %collective-permute-start.11 = (s16[272,128]{1,0:T(8,128)(2,1)S(1)}, s16[272,128]{1,0:T(8,128)(2,1)S(1)}, u32[]{:S(2)}, u32[]{:S(2)}) collective-permute-start(s16[272,128]{1,0:T(8,128)(2,1)S(1)} %get-tuple-element.25), channel_id=1, source_target_pairs={{0,3},{1,2},{2,1},{3,0},{4,7},{5,6},{6,5},{7,4},{8,11},{9,10},{10,... | collective-permute-start | bytes 208904 | tf_op jit(solution)/shard_map/ppermute | solution.py:162
  23.7 0.8 %shard_map.47.refs_9_ = f32[256,128]{1,0:T(8,128)S(1)} custom-call(s32[48]{0:T(128)S(1)} %copy-done.1, bf16[6,128,128]{2,1,0:T(8,128)(2,1)S(1)} %bitcast.22, bf16[6,128,128]{2,1,0:T(8,128)(2,1)S(1)} %collective-permute-done.2.refs_1_, bf16[6,128,128]{2,1,0:T(8,128)(2,1)S(1)} %collective-permute-done.refs_2_, ...), custom_call_target="tpu_custom_call" | custom-call | flops 100000000 | bytes 589824 | tf_op jit(solution)/shard_map/pallas_call | solution.py:116
  24.6 0.0 collective-permute-done.1.refs_0_
  24.6 0.9 %shard_map.48 = f32[256,128]{1,0:T(8,128)S(1)} custom-call(s32[48]{0:T(128)S(1)} %copy-done.1, bf16[6,128,128]{2,1,0:T(8,128)(2,1)S(1)} %collective-permute-done.1.refs_0_, bf16[3,128,128]{2,1,0:T(8,128)(2,1)S(1)} %get-tuple-element.21.refs_3_.refs_1_, bf16[3,128,128]{2,1,0:T(8,128)(2,1)S(1)} %collective-permute-done.3.refs_4_.refs_2_, ...), custom_call_target="tpu_custom_call" | custom-call | flops 99999997952 | bytes 196608 | tf_op jit(solution)/shard_map/pallas_call | solution.py:116
  25.5 1.8 %collective-permute-done.10 = s16[272,128]{1,0:T(8,128)(2,1)S(1)} collective-permute-done((s16[272,128]{1,0:T(8,128)(2,1)S(1)}, s16[272,128]{1,0:T(8,128)(2,1)S(1)}, u32[]{:S(2)}, u32[]{:S(2)}) %collective-permute-start.10) | collective-permute-done | bytes 69664 | tf_op jit(solution)/shard_map/ppermute | solution.py:162
  27.3 0.0 collective-permute-done.11
  27.3 0.7 %fusion.1 = bf16[256,128]{1,0:T(8,128)(2,1)} fusion(f32[256,128]{1,0:T(8,128)S(1)} %shard_map.48, f32[2,128]{1,0:T(2,128)S(1)} %get-tuple-element.31, s16[272,128]{1,0:T(8,128)(2,1)S(1)} %collective-permute-done.11, f32[2,128]{1,0:T(2,128)S(1)} %get-tuple-element.32, s16[272,128]{1,0:T(8,128)(2,1)S(1)} %collective-permute-done.10), kind=kLoop, calls=%fused_computation.2 | loop fusion | flops 229376 | bytes 329728 | tf_op jit(solution)/shard_map/convert_element_type | solution.py:225
  (1 shorter events, 0.0 us)
Async XLA Ops:
  0.0 13.5 %collective-permute-start = (bf16[6,128,128]{2,1,0:T(8,128)(2,1)}, bf16[6,128,128]{2,1,0:T(8,128)(2,1)S(1)}, u32[]{:S(2)}, u32[]{:S(2)}) collective-permute-start(bf16[6,128,128]{2,1,0:T(8,128)(2,1)} %bitcast.19), channel_id=1, source_target_pairs={{0,4},{1,5},{2,6},{3,7},{4,0},{5,1},{6,2},{7,3},{8,12},{9,13},{10,... | collective-permute-start | bytes 589832 | tf_op jit(solution)/shard_map/ppermute | solution.py:162
  4.0 1.0 %copy-start = (bf16[1,1,6,128,128]{4,3,2,1,0:T(8,128)(2,1)S(1)}, bf16[1,1,6,128,128]{4,3,2,1,0:T(8,128)(2,1)}, u32[]{:S(2)}) copy-start(bf16[1,1,6,128,128]{4,3,2,1,0:T(8,128)(2,1)} %param.4) | copy-start | bytes 589828
  5.1 12.7 %collective-permute-start.2 = (bf16[6,128,128]{2,1,0:T(8,128)(2,1)S(1)}, bf16[6,128,128]{2,1,0:T(8,128)(2,1)S(1)}, u32[]{:S(2)}, u32[]{:S(2)}) collective-permute-start(bf16[6,128,128]{2,1,0:T(8,128)(2,1)S(1)} %bitcast.20), channel_id=1, source_target_pairs={{0,2},{1,3},{2,0},{3,1},{4,6},{5,7},{6,4},{7,5},{8,10},{9,11},{10,... | collective-permute-start | bytes 589832 | tf_op jit(solution)/shard_map/ppermute | solution.py:162
  6.7 7.6 %collective-permute-start.6 = (bf16[3,128,128]{2,1,0:T(8,128)(2,1)S(1)}, bf16[3,128,128]{2,1,0:T(8,128)(2,1)S(1)}, u32[]{:S(2)}, u32[]{:S(2)}) collective-permute-start(bf16[3,128,128]{2,1,0:T(8,128)(2,1)S(1)} %get-tuple-element.21.refs_3_.refs_1_), channel_id=1, source_target_pairs={{0,16},{8,24},{16,0},{24,8},{1,17},{9,25},{17,1},{25,9},{2,18},{10... | collective-permute-start | bytes 294920 | tf_op jit(solution)/shard_map/ppermute | solution.py:162
  8.2 6.1 %collective-permute-start.7 = (bf16[3,128,128]{2,1,0:T(8,128)(2,1)S(1)}, bf16[3,128,128]{2,1,0:T(8,128)(2,1)S(1)}, u32[]{:S(2)}, u32[]{:S(2)}) collective-permute-start(bf16[3,128,128]{2,1,0:T(8,128)(2,1)S(1)} %get-tuple-element.22), channel_id=1, source_target_pairs={{17,0},{16,1},{25,2},{24,3},{21,4},{20,5},{23,6},{22,7},{19,8},{18... | collective-permute-start | bytes 294920 | tf_op jit(solution)/shard_map/ppermute | solution.py:172
  9.7 8.1 %collective-permute-start.3 = (bf16[3,128,128]{2,1,0:T(8,128)(2,1)S(1)}, bf16[3,128,128]{2,1,0:T(8,128)(2,1)S(1)}, u32[]{:S(2)}, u32[]{:S(2)}) collective-permute-start(bf16[3,128,128]{2,1,0:T(8,128)(2,1)S(1)} %get-tuple-element.22), channel_id=1, source_target_pairs={{1,0},{0,1},{3,2},{2,3},{5,4},{4,5},{13,6},{12,7},{9,8},{8,9},{11,... | collective-permute-start | bytes 294920 | tf_op jit(solution)/shard_map/ppermute | solution.py:172
  13.5 11.1 %collective-permute-start.1 = (bf16[6,128,128]{2,1,0:T(8,128)(2,1)S(1)}, bf16[6,128,128]{2,1,0:T(8,128)(2,1)S(1)}, u32[]{:S(2)}, u32[]{:S(2)}) collective-permute-start(bf16[6,128,128]{2,1,0:T(8,128)(2,1)S(1)} %collective-permute-done.refs_2_), channel_id=1, source_target_pairs={{0,2},{1,3},{2,0},{3,1},{4,6},{5,7},{6,4},{7,5},{8,10},{9,11},{10,... | collective-permute-start | bytes 589832 | tf_op jit(solution)/shard_map/ppermute | solution.py:162
  14.2 4.1 %collective-permute-start.8 = (bf16[3,128,128]{2,1,0:T(8,128)(2,1)S(1)}, bf16[3,128,128]{2,1,0:T(8,128)(2,1)S(1)}, u32[]{:S(2)}, u32[]{:S(2)}) collective-permute-start(bf16[3,128,128]{2,1,0:T(8,128)(2,1)S(1)} %collective-permute-done.6.refs_7_.refs_5_), channel_id=1, source_target_pairs={{0,8},{8,0},{16,24},{24,16},{1,9},{9,1},{17,25},{25,17},{2,10},{10... | collective-permute-start | bytes 294920 | tf_op jit(solution)/shard_map/ppermute | solution.py:162
  14.2 4.5 %collective-permute-start.9 = (bf16[3,128,128]{2,1,0:T(8,128)(2,1)S(1)}, bf16[3,128,128]{2,1,0:T(8,128)(2,1)S(1)}, u32[]{:S(2)}, u32[]{:S(2)}) collective-permute-start(bf16[3,128,128]{2,1,0:T(8,128)(2,1)S(1)} %collective-permute-done.7.refs_8_.refs_6_), channel_id=1, source_target_pairs={{0,8},{8,0},{16,24},{24,16},{1,9},{9,1},{17,25},{25,17},{2,10},{10... | collective-permute-start | bytes 294920 | tf_op jit(solution)/shard_map/ppermute | solution.py:162
  17.8 1.3 %collective-permute-start.5 = (bf16[3,128,128]{2,1,0:T(8,128)(2,1)S(1)}, bf16[3,128,128]{2,1,0:T(8,128)(2,1)S(1)}, u32[]{:S(2)}, u32[]{:S(2)}) collective-permute-start(bf16[3,128,128]{2,1,0:T(8,128)(2,1)S(1)} %collective-permute-done.3.refs_4_.refs_2_), channel_id=1, source_target_pairs={{0,8},{8,0},{16,24},{24,16},{1,9},{9,1},{17,25},{25,17},{2,10},{10... | collective-permute-start | bytes 294920 | tf_op jit(solution)/shard_map/ppermute | solution.py:162
  17.8 1.5 %collective-permute-start.4 = (bf16[3,128,128]{2,1,0:T(8,128)(2,1)S(1)}, bf16[3,128,128]{2,1,0:T(8,128)(2,1)S(1)}, u32[]{:S(2)}, u32[]{:S(2)}) collective-permute-start(bf16[3,128,128]{2,1,0:T(8,128)(2,1)S(1)} %get-tuple-element.21.refs_3_.refs_1_), channel_id=1, source_target_pairs={{0,8},{8,0},{16,24},{24,16},{1,9},{9,1},{17,25},{25,17},{2,10},{10... | collective-permute-start | bytes 294920 | tf_op jit(solution)/shard_map/ppermute | solution.py:162
  19.2 0.7 %copy-start.1 = (s32[48]{0:T(128)S(1)}, s32[48]{0:T(128)}, u32[]{:S(2)}) copy-start(s32[48]{0:T(128)} %shard_map.46.codes_ref) | copy-start | bytes 580
  21.4 5.9 %collective-permute-start.10 = (s16[272,128]{1,0:T(8,128)(2,1)S(1)}, s16[272,128]{1,0:T(8,128)(2,1)S(1)}, u32[]{:S(2)}, u32[]{:S(2)}) collective-permute-start(s16[272,128]{1,0:T(8,128)(2,1)S(1)} %get-tuple-element.24), channel_id=1, source_target_pairs={{0,1},{1,0},{2,3},{3,2},{4,5},{5,4},{6,7},{7,6},{8,9},{9,8},{10,11... | collective-permute-start | bytes 208904 | tf_op jit(solution)/shard_map/ppermute | solution.py:162
  22.0 5.3 %collective-permute-start.11 = (s16[272,128]{1,0:T(8,128)(2,1)S(1)}, s16[272,128]{1,0:T(8,128)(2,1)S(1)}, u32[]{:S(2)}, u32[]{:S(2)}) collective-permute-start(s16[272,128]{1,0:T(8,128)(2,1)S(1)} %get-tuple-element.25), channel_id=1, source_target_pairs={{0,3},{1,2},{2,1},{3,0},{4,7},{5,6},{6,5},{7,4},{8,11},{9,10},{10,... | collective-permute-start | bytes 208904 | tf_op jit(solution)/shard_map/ppermute | solution.py:162

commit v2 on v1

--- a/solution.py
+++ b/solution.py
@@ -204,12 +204,12 @@
     codes = find_matches(left_index, right_index)
     given = lax.dynamic_index_in_dim(right, 1 - y, 0, keepdims=False)
     own = lax.dynamic_index_in_dim(right, y, 0, keepdims=False)
-    lefts, codes, (own, given) = gather(left, codes, (own, given))
+    pairs = []
+    for t in range(0, lax.axis_size("row"), 2):
+        pairs.append([across(own, "row", t) if t else own, other_half(given, t)])
+    lefts, codes, pairs[-1][0] = gather(left, codes, pairs[-1][0])
     rights = []
-    for t in range(0, lax.axis_size("row"), 2):
-        pair = [across(own, "row", t) if t else own, other_half(given, t)]
-        if not t:
-            pair[0], lefts[1] = lax.optimization_barrier((pair[0], lefts[1]))
+    for pair in pairs:
         rights += pair + [across(half, "row", 1) for half in pair]
 
     plain = jax.ShapeDtypeStruct((RT * tile, tile), jnp.float32)

time: 28.3 us -> 28.2 us (level)
  the two profiles are of different devices: /device:TPU:0 before, /device:TPU:6 now
where the time goes in v2:
time: 28.2 us; the launch traced here: 28.1 us
  starting transfers between devices  11.9 us (42%)
  waiting for transfers between devices  8.34 us (30%)
  Pallas kernels  5.43 us (19%)
  local copies, waits for them, and re-layouts  1.65 us (6%)
  other arithmetic  0.7 us (2%)
    ppermute x10, starting transfers between devices, across(): return lax.ppermute(block, axis, route)  8.97 us
    ppermute x10, waiting for transfers between devices, across(): return lax.ppermute(block, axis, route)  8.33 us
    pallas_call x3, Pallas kernels, products(): pl.pallas_call(kernel, out_shape=[out_shape] * len(sides), in_specs=[SMEM...  3.13 us
    ppermute x2, starting transfers between devices, travel(): return lax.ppermute(block, ('row', 'col'), route)  2.95 us
    pallas_call x1, Pallas kernels, find_matches(): pl.pallas_call(kernel, out_shape=jax.ShapeDtypeStruct((total,), jnp.int32...  2.3 us
    squeeze x1, local copies, waits for them, and re-layouts, shards(): given = lax.dynamic_index_in_dim(right, 1 - y, 0, keepdims=False)  0.99 us
    convert_element_type x1, other arithmetic, shards(): return (mine + decoded(coming) + decoded(from_far)).astype(jnp.bfloat16)  0.69 us
    unnamed x4, local copies, waits for them, and re-layouts  0.66 us
  transfers between devices with their start and end apart: 12, of which 6 were waited for; matrix products, arithmetic and copies ran while one was open for 4% of the time, Pallas kernels for 19%

profile of v2, /device:TPU:6, one launch (start us, length us, event | category | flops | bytes accessed | tf_op | source)
XLA Modules:
  0.0 28.1 jit_solution(2969609276234256401)
XLA Ops:
  0.0 2.6 %collective-permute-start = (bf16[6,128,128]{2,1,0:T(8,128)(2,1)}, bf16[6,128,128]{2,1,0:T(8,128)(2,1)S(1)}, u32[]{:S(2)}, u32[]{:S(2)}) collective-permute-start(bf16[6,128,128]{2,1,0:T(8,128)(2,1)} %bitcast.19), channel_id=1, source_target_pairs={{0,4},{1,5},{2,6},{3,7},{4,0},{5,1},{6,2},{7,3},{8,12},{9,13},{10,... | collective-permute-start | bytes 589832 | tf_op jit(solution)/shard_map/ppermute | solution.py:162
  2.6 0.0 copy-start
  2.6 1.0 %dynamic-slice_bitcast_fusion = (bf16[3,128,128]{2,1,0:T(8,128)(2,1)S(1)}, bf16[3,128,128]{2,1,0:T(8,128)(2,1)S(1)}) fusion(bf16[1,1,2,3,128,128]{5,4,3,2,1,0:T(8,128)(2,1)} %param.6, s32[]{:T(128)S(6)} %select_n.8, s32[]{:T(128)S(6)} %select_n.7), kind=kLoop, calls=%fused_computation.5 | loop fusion | bytes 393224 | tf_op jit(solution)/shard_map/jit(dynamic_index_in_dim)/squeeze | solution.py:205
  3.6 0.6 %collective-permute-start.5 = (bf16[3,128,128]{2,1,0:T(8,128)(2,1)S(1)}, bf16[3,128,128]{2,1,0:T(8,128)(2,1)S(1)}, u32[]{:S(2)}, u32[]{:S(2)}) collective-permute-start(bf16[3,128,128]{2,1,0:T(8,128)(2,1)S(1)} %get-tuple-element.24.refs_3_.refs_1_), channel_id=1, source_target_pairs={{0,16},{8,24},{16,0},{24,8},{1,17},{9,25},{17,1},{25,9},{2,18},{10... | collective-permute-start | bytes 294920 | tf_op jit(solution)/shard_map/ppermute | solution.py:162
  4.2 1.4 %collective-permute-start.6 = (bf16[3,128,128]{2,1,0:T(8,128)(2,1)S(1)}, bf16[3,128,128]{2,1,0:T(8,128)(2,1)S(1)}, u32[]{:S(2)}, u32[]{:S(2)}) collective-permute-start(bf16[3,128,128]{2,1,0:T(8,128)(2,1)S(1)} %get-tuple-element.23), channel_id=1, source_target_pairs={{17,0},{16,1},{25,2},{24,3},{21,4},{20,5},{23,6},{22,7},{19,8},{18... | collective-permute-start | bytes 294920 | tf_op jit(solution)/shard_map/ppermute | solution.py:172
  5.6 1.5 %collective-permute-start.2 = (bf16[3,128,128]{2,1,0:T(8,128)(2,1)S(1)}, bf16[3,128,128]{2,1,0:T(8,128)(2,1)S(1)}, u32[]{:S(2)}, u32[]{:S(2)}) collective-permute-start(bf16[3,128,128]{2,1,0:T(8,128)(2,1)S(1)} %get-tuple-element.23), channel_id=1, source_target_pairs={{1,0},{0,1},{3,2},{2,3},{5,4},{4,5},{13,6},{12,7},{9,8},{8,9},{11,... | collective-permute-start | bytes 294920 | tf_op jit(solution)/shard_map/ppermute | solution.py:172
  7.1 0.0 collective-permute-start.3
  7.1 1.8 %collective-permute-done.5.refs_7_.refs_5_ = bf16[3,128,128]{2,1,0:T(8,128)(2,1)S(1)} collective-permute-done((bf16[3,128,128]{2,1,0:T(8,128)(2,1)S(1)}, bf16[3,128,128]{2,1,0:T(8,128)(2,1)S(1)}, u32[]{:S(2)}, u32[]{:S(2)}) %collective-permute-start.5) | collective-permute-done | bytes 98336 | tf_op jit(solution)/shard_map/ppermute | solution.py:162
  9.0 0.0 copy-done
  9.0 1.6 %collective-permute-start.9 = (bf16[6,128,128]{2,1,0:T(8,128)(2,1)S(1)}, bf16[6,128,128]{2,1,0:T(8,128)(2,1)S(1)}, u32[]{:S(2)}, u32[]{:S(2)}) collective-permute-start(bf16[6,128,128]{2,1,0:T(8,128)(2,1)S(1)} %bitcast.20), channel_id=1, source_target_pairs={{0,2},{1,3},{2,0},{3,1},{4,6},{5,7},{6,4},{7,5},{8,10},{9,11},{10,... | collective-permute-start | bytes 589832 | tf_op jit(solution)/shard_map/ppermute | solution.py:162
  10.5 2.3 %shard_map.46.codes_ref = s32[48]{0:T(128)} custom-call(s32[6,4,8]{2,1,0:T(4,128)} %bitcast.23, s32[4,3,2,8]{3,2,1,0:T(2,128)} %bitcast.24), custom_call_target="tpu_custom_call" | custom-call | tf_op jit(solution)/shard_map/pallas_call | solution.py:61
  12.9 0.0 collective-permute-done.refs_2_
  12.9 0.5 %collective-permute-start.1 = (bf16[6,128,128]{2,1,0:T(8,128)(2,1)S(1)}, bf16[6,128,128]{2,1,0:T(8,128)(2,1)S(1)}, u32[]{:S(2)}, u32[]{:S(2)}) collective-permute-start(bf16[6,128,128]{2,1,0:T(8,128)(2,1)S(1)} %collective-permute-done.refs_2_), channel_id=1, source_target_pairs={{0,2},{1,3},{2,0},{3,1},{4,6},{5,7},{6,4},{7,5},{8,10},{9,11},{10,... | collective-permute-start | bytes 589832 | tf_op jit(solution)/shard_map/ppermute | solution.py:162
  13.4 0.0 collective-permute-done.6.refs_8_.refs_6_
  13.4 0.0 collective-permute-start.8
  13.4 0.0 collective-permute-done.2.refs_4_.refs_2_
  13.4 1.7 %collective-permute-start.4 = (bf16[3,128,128]{2,1,0:T(8,128)(2,1)S(1)}, bf16[3,128,128]{2,1,0:T(8,128)(2,1)S(1)}, u32[]{:S(2)}, u32[]{:S(2)}) collective-permute-start(bf16[3,128,128]{2,1,0:T(8,128)(2,1)S(1)} %collective-permute-done.2.refs_4_.refs_2_), channel_id=1, source_target_pairs={{0,8},{8,0},{16,24},{24,16},{1,9},{9,1},{17,25},{25,17},{2,10},{10... | collective-permute-start | bytes 294920 | tf_op jit(solution)/shard_map/ppermute | solution.py:162
  15.1 0.0 collective-permute-done.3.refs_5_.refs_3_
  15.1 0.0 collective-permute-start.7
  15.1 0.0 collective-permute-done.8.refs_10_.refs_8_
  15.1 0.9 %collective-permute-done.4.refs_6_.refs_4_ = bf16[3,128,128]{2,1,0:T(8,128)(2,1)S(1)} collective-permute-done((bf16[3,128,128]{2,1,0:T(8,128)(2,1)S(1)}, bf16[3,128,128]{2,1,0:T(8,128)(2,1)S(1)}, u32[]{:S(2)}, u32[]{:S(2)}) %collective-permute-start.4) | collective-permute-done | bytes 98336 | tf_op jit(solution)/shard_map/ppermute | solution.py:162
  16.0 0.4 %collective-permute-done.7.refs_9_.refs_7_ = bf16[3,128,128]{2,1,0:T(8,128)(2,1)S(1)} collective-permute-done((bf16[3,128,128]{2,1,0:T(8,128)(2,1)S(1)}, bf16[3,128,128]{2,1,0:T(8,128)(2,1)S(1)}, u32[]{:S(2)}, u32[]{:S(2)}) %collective-permute-start.7) | collective-permute-done | bytes 98336 | tf_op jit(solution)/shard_map/ppermute | solution.py:162
  16.4 1.9 %collective-permute-done.9.refs_1_ = bf16[6,128,128]{2,1,0:T(8,128)(2,1)S(1)} collective-permute-done((bf16[6,128,128]{2,1,0:T(8,128)(2,1)S(1)}, bf16[6,128,128]{2,1,0:T(8,128)(2,1)S(1)}, u32[]{:S(2)}, u32[]{:S(2)}) %collective-permute-start.9) | collective-permute-done | bytes 196640 | tf_op jit(solution)/shard_map/ppermute | solution.py:162
  18.3 0.0 copy-start.1
  18.3 0.7 %copy-done.1 = s32[48]{0:T(128)S(1)} copy-done((s32[48]{0:T(128)S(1)}, s32[48]{0:T(128)}, u32[]{:S(2)}) %copy-start.1) | copy-done | bytes 216
  19.0 1.2 %shard_map.49 = (s16[272,128]{1,0:T(8,128)(2,1)S(1)}, s16[272,128]{1,0:T(8,128)(2,1)S(1)}) custom-call(s32[48]{0:T(128)S(1)} %copy-done.1, bf16[6,128,128]{2,1,0:T(8,128)(2,1)S(1)} %bitcast.21, bf16[6,128,128]{2,1,0:T(8,128)(2,1)S(1)} %collective-permute-done.9.refs_1_, bf16[6,128,128]{2,1,0:T(8,128)(2,1)S(1)} %collective-permute-done.refs_2_, ...), custom_call_target="tpu_custom_call" | custom-call | flops 100000000 | bytes 589824 | tf_op jit(solution)/shard_map/pallas_call | solution.py:116
  20.2 2.0 %collective-permute-start.10 = (s16[272,128]{1,0:T(8,128)(2,1)S(1)}, s16[272,128]{1,0:T(8,128)(2,1)S(1)}, u32[]{:S(2)}, u32[]{:S(2)}) collective-permute-start(s16[272,128]{1,0:T(8,128)(2,1)S(1)} %get-tuple-element.18), channel_id=1, source_target_pairs={{0,1},{1,0},{2,3},{3,2},{4,5},{5,4},{6,7},{7,6},{8,9},{9,8},{10,11... | collective-permute-start | bytes 208904 | tf_op jit(solution)/shard_map/ppermute | solution.py:162
  22.2 0.0 collective-permute-start.11
  22.2 1.1 %shard_map.47.refs_9_ = f32[256,128]{1,0:T(8,128)S(1)} custom-call(s32[48]{0:T(128)S(1)} %copy-done.1, bf16[6,128,128]{2,1,0:T(8,128)(2,1)S(1)} %bitcast.22, bf16[6,128,128]{2,1,0:T(8,128)(2,1)S(1)} %collective-permute-done.9.refs_1_, bf16[6,128,128]{2,1,0:T(8,128)(2,1)S(1)} %collective-permute-done.refs_2_, ...), custom_call_target="tpu_custom_call" | custom-call | flops 100000000 | bytes 589824 | tf_op jit(solution)/shard_map/pallas_call | solution.py:116
  23.3 0.0 collective-permute-done.1.refs_0_
  23.3 0.8 %shard_map.48 = f32[256,128]{1,0:T(8,128)S(1)} custom-call(s32[48]{0:T(128)S(1)} %copy-done.1, bf16[6,128,128]{2,1,0:T(8,128)(2,1)S(1)} %collective-permute-done.1.refs_0_, bf16[3,128,128]{2,1,0:T(8,128)(2,1)S(1)} %get-tuple-element.24.refs_3_.refs_1_, bf16[3,128,128]{2,1,0:T(8,128)(2,1)S(1)} %collective-permute-done.2.refs_4_.refs_2_, ...), custom_call_target="tpu_custom_call" | custom-call | flops 99999997952 | bytes 196608 | tf_op jit(solution)/shard_map/pallas_call | solution.py:116
  24.1 0.5 %collective-permute-done.10 = s16[272,128]{1,0:T(8,128)(2,1)S(1)} collective-permute-done((s16[272,128]{1,0:T(8,128)(2,1)S(1)}, s16[272,128]{1,0:T(8,128)(2,1)S(1)}, u32[]{:S(2)}, u32[]{:S(2)}) %collective-permute-start.10) | collective-permute-done | bytes 69664 | tf_op jit(solution)/shard_map/ppermute | solution.py:162
  24.6 2.8 %collective-permute-done.11 = s16[272,128]{1,0:T(8,128)(2,1)S(1)} collective-permute-done((s16[272,128]{1,0:T(8,128)(2,1)S(1)}, s16[272,128]{1,0:T(8,128)(2,1)S(1)}, u32[]{:S(2)}, u32[]{:S(2)}) %collective-permute-start.11) | collective-permute-done | bytes 69664 | tf_op jit(solution)/shard_map/ppermute | solution.py:162
  27.4 0.7 %fusion.1 = bf16[256,128]{1,0:T(8,128)(2,1)} fusion(f32[256,128]{1,0:T(8,128)S(1)} %shard_map.48, f32[2,128]{1,0:T(2,128)S(1)} %get-tuple-element.25, s16[272,128]{1,0:T(8,128)(2,1)S(1)} %collective-permute-done.11, f32[2,128]{1,0:T(2,128)S(1)} %get-tuple-element.26, s16[272,128]{1,0:T(8,128)(2,1)S(1)} %collective-permute-done.10), kind=kLoop, calls=%fused_computation.2 | loop fusion | flops 229376 | bytes 329728 | tf_op jit(solution)/shard_map/convert_element_type | solution.py:225
  (1 shorter events, 0.0 us)
Async XLA Ops:
  0.0 12.9 %collective-permute-start = (bf16[6,128,128]{2,1,0:T(8,128)(2,1)}, bf16[6,128,128]{2,1,0:T(8,128)(2,1)S(1)}, u32[]{:S(2)}, u32[]{:S(2)}) collective-permute-start(bf16[6,128,128]{2,1,0:T(8,128)(2,1)} %bitcast.19), channel_id=1, source_target_pairs={{0,4},{1,5},{2,6},{3,7},{4,0},{5,1},{6,2},{7,3},{8,12},{9,13},{10,... | collective-permute-start | bytes 589832 | tf_op jit(solution)/shard_map/ppermute | solution.py:162
  2.6 6.4 %copy-start = (bf16[1,1,6,128,128]{4,3,2,1,0:T(8,128)(2,1)S(1)}, bf16[1,1,6,128,128]{4,3,2,1,0:T(8,128)(2,1)}, u32[]{:S(2)}) copy-start(bf16[1,1,6,128,128]{4,3,2,1,0:T(8,128)(2,1)} %param.4) | copy-start | bytes 589828
  3.6 5.4 %collective-permute-start.5 = (bf16[3,128,128]{2,1,0:T(8,128)(2,1)S(1)}, bf16[3,128,128]{2,1,0:T(8,128)(2,1)S(1)}, u32[]{:S(2)}, u32[]{:S(2)}) collective-permute-start(bf16[3,128,128]{2,1,0:T(8,128)(2,1)S(1)} %get-tuple-element.24.refs_3_.refs_1_), channel_id=1, source_target_pairs={{0,16},{8,24},{16,0},{24,8},{1,17},{9,25},{17,1},{25,9},{2,18},{10... | collective-permute-start | bytes 294920 | tf_op jit(solution)/shard_map/ppermute | solution.py:162
  4.2 9.2 %collective-permute-start.6 = (bf16[3,128,128]{2,1,0:T(8,128)(2,1)S(1)}, bf16[3,128,128]{2,1,0:T(8,128)(2,1)S(1)}, u32[]{:S(2)}, u32[]{:S(2)}) collective-permute-start(bf16[3,128,128]{2,1,0:T(8,128)(2,1)S(1)} %get-tuple-element.23), channel_id=1, source_target_pairs={{17,0},{16,1},{25,2},{24,3},{21,4},{20,5},{23,6},{22,7},{19,8},{18... | collective-permute-start | bytes 294920 | tf_op jit(solution)/shard_map/ppermute | solution.py:172
  5.6 7.8 %collective-permute-start.2 = (bf16[3,128,128]{2,1,0:T(8,128)(2,1)S(1)}, bf16[3,128,128]{2,1,0:T(8,128)(2,1)S(1)}, u32[]{:S(2)}, u32[]{:S(2)}) collective-permute-start(bf16[3,128,128]{2,1,0:T(8,128)(2,1)S(1)} %get-tuple-element.23), channel_id=1, source_target_pairs={{1,0},{0,1},{3,2},{2,3},{5,4},{4,5},{13,6},{12,7},{9,8},{8,9},{11,... | collective-permute-start | bytes 294920 | tf_op jit(solution)/shard_map/ppermute | solution.py:172
  7.1 7.9 %collective-permute-start.3 = (bf16[3,128,128]{2,1,0:T(8,128)(2,1)S(1)}, bf16[3,128,128]{2,1,0:T(8,128)(2,1)S(1)}, u32[]{:S(2)}, u32[]{:S(2)}) collective-permute-start(bf16[3,128,128]{2,1,0:T(8,128)(2,1)S(1)} %get-tuple-element.24.refs_3_.refs_1_), channel_id=1, source_target_pairs={{0,8},{8,0},{16,24},{24,16},{1,9},{9,1},{17,25},{25,17},{2,10},{10... | collective-permute-start | bytes 294920 | tf_op jit(solution)/shard_map/ppermute | solution.py:162
  9.0 9.3 %collective-permute-start.9 = (bf16[6,128,128]{2,1,0:T(8,128)(2,1)S(1)}, bf16[6,128,128]{2,1,0:T(8,128)(2,1)S(1)}, u32[]{:S(2)}, u32[]{:S(2)}) collective-permute-start(bf16[6,128,128]{2,1,0:T(8,128)(2,1)S(1)} %bitcast.20), channel_id=1, source_target_pairs={{0,2},{1,3},{2,0},{3,1},{4,6},{5,7},{6,4},{7,5},{8,10},{9,11},{10,... | collective-permute-start | bytes 589832 | tf_op jit(solution)/shard_map/ppermute | solution.py:162
  12.9 10.4 %collective-permute-start.1 = (bf16[6,128,128]{2,1,0:T(8,128)(2,1)S(1)}, bf16[6,128,128]{2,1,0:T(8,128)(2,1)S(1)}, u32[]{:S(2)}, u32[]{:S(2)}) collective-permute-start(bf16[6,128,128]{2,1,0:T(8,128)(2,1)S(1)} %collective-permute-done.refs_2_), channel_id=1, source_target_pairs={{0,2},{1,3},{2,0},{3,1},{4,6},{5,7},{6,4},{7,5},{8,10},{9,11},{10,... | collective-permute-start | bytes 589832 | tf_op jit(solution)/shard_map/ppermute | solution.py:162
  13.4 1.7 %collective-permute-start.8 = (bf16[3,128,128]{2,1,0:T(8,128)(2,1)S(1)}, bf16[3,128,128]{2,1,0:T(8,128)(2,1)S(1)}, u32[]{:S(2)}, u32[]{:S(2)}) collective-permute-start(bf16[3,128,128]{2,1,0:T(8,128)(2,1)S(1)} %collective-permute-done.6.refs_8_.refs_6_), channel_id=1, source_target_pairs={{0,8},{8,0},{16,24},{24,16},{1,9},{9,1},{17,25},{25,17},{2,10},{10... | collective-permute-start | bytes 294920 | tf_op jit(solution)/shard_map/ppermute | solution.py:162
  13.4 2.6 %collective-permute-start.4 = (bf16[3,128,128]{2,1,0:T(8,128)(2,1)S(1)}, bf16[3,128,128]{2,1,0:T(8,128)(2,1)S(1)}, u32[]{:S(2)}, u32[]{:S(2)}) collective-permute-start(bf16[3,128,128]{2,1,0:T(8,128)(2,1)S(1)} %collective-permute-done.2.refs_4_.refs_2_), channel_id=1, source_target_pairs={{0,8},{8,0},{16,24},{24,16},{1,9},{9,1},{17,25},{25,17},{2,10},{10... | collective-permute-start | bytes 294920 | tf_op jit(solution)/shard_map/ppermute | solution.py:162
  15.1 1.3 %collective-permute-start.7 = (bf16[3,128,128]{2,1,0:T(8,128)(2,1)S(1)}, bf16[3,128,128]{2,1,0:T(8,128)(2,1)S(1)}, u32[]{:S(2)}, u32[]{:S(2)}) collective-permute-start(bf16[3,128,128]{2,1,0:T(8,128)(2,1)S(1)} %collective-permute-done.5.refs_7_.refs_5_), channel_id=1, source_target_pairs={{0,8},{8,0},{16,24},{24,16},{1,9},{9,1},{17,25},{25,17},{2,10},{10... | collective-permute-start | bytes 294920 | tf_op jit(solution)/shard_map/ppermute | solution.py:162
  18.3 0.7 %copy-start.1 = (s32[48]{0:T(128)S(1)}, s32[48]{0:T(128)}, u32[]{:S(2)}) copy-start(s32[48]{0:T(128)} %shard_map.46.codes_ref) | copy-start | bytes 580
  20.2 4.4 %collective-permute-start.10 = (s16[272,128]{1,0:T(8,128)(2,1)S(1)}, s16[272,128]{1,0:T(8,128)(2,1)S(1)}, u32[]{:S(2)}, u32[]{:S(2)}) collective-permute-start(s16[272,128]{1,0:T(8,128)(2,1)S(1)} %get-tuple-element.18), channel_id=1, source_target_pairs={{0,1},{1,0},{2,3},{3,2},{4,5},{5,4},{6,7},{7,6},{8,9},{9,8},{10,11... | collective-permute-start | bytes 208904 | tf_op jit(solution)/shard_map/ppermute | solution.py:162
  22.2 5.2 %collective-permute-start.11 = (s16[272,128]{1,0:T(8,128)(2,1)S(1)}, s16[272,128]{1,0:T(8,128)(2,1)S(1)}, u32[]{:S(2)}, u32[]{:S(2)}) collective-permute-start(s16[272,128]{1,0:T(8,128)(2,1)S(1)} %get-tuple-element.19), channel_id=1, source_target_pairs={{0,3},{1,2},{2,1},{3,0},{4,7},{5,6},{6,5},{7,4},{8,11},{9,10},{10,... | collective-permute-start | bytes 208904 | tf_op jit(solution)/shard_map/ppermute | solution.py:162

commit v3 on v2

--- a/solution.py
+++ b/solution.py
@@ -23,8 +23,7 @@
 
 
 def counting(side, places):
-    early = [s for s in range(places) if s % 2 == 0 or s == 1]
-    return [range(places), early, [s for s in early if s > 1]][side]
+    return range(0, places, 2 if side else 1)
 
 
 def code_at(s, side, places, slots):
@@ -174,9 +173,8 @@
 
 def other_half(given, t):
     def source(r, z, y):
-        apart = r ^ t ^ z
-        swap = apart % 2 if apart > 1 else 0
-        return r ^ t ^ swap, z ^ swap, y ^ 1
+        odd = (r ^ t ^ z) & 1
+        return r ^ t ^ odd, z ^ odd, y ^ 1
 
     return travel(given, source)
 

time: 28.2 us -> 27 us (0.957)
  the two profiles are of different devices: /device:TPU:6 before, /device:TPU:0 now
where the time goes in v3:
time: 27 us; the launch traced here: 26.7 us
  starting transfers between devices  14.3 us (53%)
  Pallas kernels  5.35 us (20%)
  waiting for transfers between devices  4.63 us (17%)
  local copies, waits for them, and re-layouts  1.65 us (6%)
  other arithmetic  0.71 us (3%)
    ppermute x10, starting transfers between devices, across(): return lax.ppermute(block, axis, route)  12.3 us
    ppermute x10, waiting for transfers between devices, across(): return lax.ppermute(block, axis, route)  4.52 us
    pallas_call x3, Pallas kernels, products(): pl.pallas_call(kernel, out_shape=[out_shape] * len(sides), in_specs=[SMEM...  3.04 us
    pallas_call x1, Pallas kernels, find_matches(): pl.pallas_call(kernel, out_shape=jax.ShapeDtypeStruct((total,), jnp.int32...  2.3 us
    ppermute x2, starting transfers between devices, travel(): return lax.ppermute(block, ('row', 'col'), route)  2 us
    squeeze x1, local copies, waits for them, and re-layouts, shards(): given = lax.dynamic_index_in_dim(right, 1 - y, 0, keepdims=False)  0.99 us
    convert_element_type x1, other arithmetic, shards(): return (mine + decoded(coming) + decoded(from_far)).astype(jnp.bfloat16)  0.69 us
    unnamed x4, local copies, waits for them, and re-layouts  0.66 us
  transfers between devices with their start and end apart: 12, of which 5 were waited for; matrix products, arithmetic and copies ran while one was open for 4% of the time, Pallas kernels for 20%

profile of v3, /device:TPU:0, one launch (start us, length us, event | category | flops | bytes accessed | tf_op | source)
XLA Modules:
  0.0 26.7 jit_solution(13502355886647750911)
XLA Ops:
  0.0 4.0 %collective-permute-start = (bf16[6,128,128]{2,1,0:T(8,128)(2,1)}, bf16[6,128,128]{2,1,0:T(8,128)(2,1)S(1)}, u32[]{:S(2)}, u32[]{:S(2)}) collective-permute-start(bf16[6,128,128]{2,1,0:T(8,128)(2,1)} %bitcast.19), channel_id=1, source_target_pairs={{0,4},{1,5},{2,6},{3,7},{4,0},{5,1},{6,2},{7,3},{8,12},{9,13},{10,... | collective-permute-start | bytes 589832 | tf_op jit(solution)/shard_map/ppermute | solution.py:161
  4.0 0.0 copy-start
  4.0 1.0 %dynamic-slice_bitcast_fusion = (bf16[3,128,128]{2,1,0:T(8,128)(2,1)S(1)}, bf16[3,128,128]{2,1,0:T(8,128)(2,1)S(1)}) fusion(bf16[1,1,2,3,128,128]{5,4,3,2,1,0:T(8,128)(2,1)} %param.6, s32[]{:T(128)S(6)} %select_n.8, s32[]{:T(128)S(6)} %select_n.7), kind=kLoop, calls=%fused_computation.5 | loop fusion | bytes 393224 | tf_op jit(solution)/shard_map/jit(dynamic_index_in_dim)/squeeze | solution.py:203
  5.0 1.6 %collective-permute-start.1 = (bf16[3,128,128]{2,1,0:T(8,128)(2,1)S(1)}, bf16[3,128,128]{2,1,0:T(8,128)(2,1)S(1)}, u32[]{:S(2)}, u32[]{:S(2)}) collective-permute-start(bf16[3,128,128]{2,1,0:T(8,128)(2,1)S(1)} %get-tuple-element.24.refs_2_), channel_id=1, source_target_pairs={{0,16},{8,24},{16,0},{24,8},{1,17},{9,25},{17,1},{25,9},{2,18},{10... | collective-permute-start | bytes 294920 | tf_op jit(solution)/shard_map/ppermute | solution.py:161
  6.6 1.5 %collective-permute-start.4 = (bf16[3,128,128]{2,1,0:T(8,128)(2,1)S(1)}, bf16[3,128,128]{2,1,0:T(8,128)(2,1)S(1)}, u32[]{:S(2)}, u32[]{:S(2)}) collective-permute-start(bf16[3,128,128]{2,1,0:T(8,128)(2,1)S(1)} %get-tuple-element.23), channel_id=1, source_target_pairs={{1,0},{0,1},{9,2},{8,3},{5,4},{4,5},{13,6},{12,7},{3,8},{2,9},{11,... | collective-permute-start | bytes 294920 | tf_op jit(solution)/shard_map/ppermute | solution.py:171
  8.1 1.1 %collective-permute-start.5 = (bf16[3,128,128]{2,1,0:T(8,128)(2,1)S(1)}, bf16[3,128,128]{2,1,0:T(8,128)(2,1)S(1)}, u32[]{:S(2)}, u32[]{:S(2)}) collective-permute-start(bf16[3,128,128]{2,1,0:T(8,128)(2,1)S(1)} %get-tuple-element.24.refs_2_), channel_id=1, source_target_pairs={{0,8},{8,0},{16,24},{24,16},{1,9},{9,1},{17,25},{25,17},{2,10},{10... | collective-permute-start | bytes 294920 | tf_op jit(solution)/shard_map/ppermute | solution.py:161
  9.2 0.5 %collective-permute-start.7 = (bf16[3,128,128]{2,1,0:T(8,128)(2,1)S(1)}, bf16[3,128,128]{2,1,0:T(8,128)(2,1)S(1)}, u32[]{:S(2)}, u32[]{:S(2)}) collective-permute-start(bf16[3,128,128]{2,1,0:T(8,128)(2,1)S(1)} %get-tuple-element.23), channel_id=1, source_target_pairs={{17,0},{16,1},{25,2},{24,3},{21,4},{20,5},{29,6},{28,7},{19,8},{18... | collective-permute-start | bytes 294920 | tf_op jit(solution)/shard_map/ppermute | solution.py:171
  9.7 2.3 %shard_map.46.codes_ref = s32[48]{0:T(128)} custom-call(s32[6,4,8]{2,1,0:T(4,128)} %bitcast.23, s32[4,3,2,8]{3,2,1,0:T(2,128)} %bitcast.24), custom_call_target="tpu_custom_call" | custom-call | tf_op jit(solution)/shard_map/pallas_call | solution.py:60
  12.0 0.0 collective-permute-done.1.refs_6_
  12.0 0.0 copy-done
  12.1 1.1 %collective-permute-start.2 = (bf16[6,128,128]{2,1,0:T(8,128)(2,1)S(1)}, bf16[6,128,128]{2,1,0:T(8,128)(2,1)S(1)}, u32[]{:S(2)}, u32[]{:S(2)}) collective-permute-start(bf16[6,128,128]{2,1,0:T(8,128)(2,1)S(1)} %bitcast.20), channel_id=1, source_target_pairs={{0,2},{1,3},{2,0},{3,1},{4,6},{5,7},{6,4},{7,5},{8,10},{9,11},{10,... | collective-permute-start | bytes 589832 | tf_op jit(solution)/shard_map/ppermute | solution.py:161
  13.2 0.3 %collective-permute-done.refs_1_ = bf16[6,128,128]{2,1,0:T(8,128)(2,1)S(1)} collective-permute-done((bf16[6,128,128]{2,1,0:T(8,128)(2,1)}, bf16[6,128,128]{2,1,0:T(8,128)(2,1)S(1)}, u32[]{:S(2)}, u32[]{:S(2)}) %collective-permute-start) | collective-permute-done | bytes 196640 | tf_op jit(solution)/shard_map/ppermute | solution.py:161
  13.5 0.8 %collective-permute-start.3 = (bf16[6,128,128]{2,1,0:T(8,128)(2,1)S(1)}, bf16[6,128,128]{2,1,0:T(8,128)(2,1)S(1)}, u32[]{:S(2)}, u32[]{:S(2)}) collective-permute-start(bf16[6,128,128]{2,1,0:T(8,128)(2,1)S(1)} %collective-permute-done.refs_1_), channel_id=1, source_target_pairs={{0,2},{1,3},{2,0},{3,1},{4,6},{5,7},{6,4},{7,5},{8,10},{9,11},{10,... | collective-permute-start | bytes 589832 | tf_op jit(solution)/shard_map/ppermute | solution.py:161
  14.2 0.0 collective-permute-done.4.refs_3_
  14.2 0.7 %collective-permute-start.8 = (bf16[3,128,128]{2,1,0:T(8,128)(2,1)S(1)}, bf16[3,128,128]{2,1,0:T(8,128)(2,1)S(1)}, u32[]{:S(2)}, u32[]{:S(2)}) collective-permute-start(bf16[3,128,128]{2,1,0:T(8,128)(2,1)S(1)} %collective-permute-done.1.refs_6_), channel_id=1, source_target_pairs={{0,8},{8,0},{16,24},{24,16},{1,9},{9,1},{17,25},{25,17},{2,10},{10... | collective-permute-start | bytes 294920 | tf_op jit(solution)/shard_map/ppermute | solution.py:161
  15.0 0.0 collective-permute-done.5.refs_4_
  15.0 0.0 collective-permute-start.6
  15.0 0.1 collective-permute-done.7.refs_7_
  15.1 1.8 %collective-permute-start.9 = (bf16[3,128,128]{2,1,0:T(8,128)(2,1)S(1)}, bf16[3,128,128]{2,1,0:T(8,128)(2,1)S(1)}, u32[]{:S(2)}, u32[]{:S(2)}) collective-permute-start(bf16[3,128,128]{2,1,0:T(8,128)(2,1)S(1)} %collective-permute-done.7.refs_7_), channel_id=1, source_target_pairs={{0,8},{8,0},{16,24},{24,16},{1,9},{9,1},{17,25},{25,17},{2,10},{10... | collective-permute-start | bytes 294920 | tf_op jit(solution)/shard_map/ppermute | solution.py:161
  16.9 0.0 collective-permute-done.6.refs_5_
  16.9 0.0 collective-permute-done.8.refs_8_
  16.9 0.9 %collective-permute-done.9.refs_9_ = bf16[3,128,128]{2,1,0:T(8,128)(2,1)S(1)} collective-permute-done((bf16[3,128,128]{2,1,0:T(8,128)(2,1)S(1)}, bf16[3,128,128]{2,1,0:T(8,128)(2,1)S(1)}, u32[]{:S(2)}, u32[]{:S(2)}) %collective-permute-start.9) | collective-permute-done | bytes 98336 | tf_op jit(solution)/shard_map/ppermute | solution.py:161
  17.9 0.0 copy-start.1
  17.9 0.7 %copy-done.1 = s32[48]{0:T(128)S(1)} copy-done((s32[48]{0:T(128)S(1)}, s32[48]{0:T(128)}, u32[]{:S(2)}) %copy-start.1) | copy-done | bytes 216
  18.5 1.3 %shard_map.49 = (s16[272,128]{1,0:T(8,128)(2,1)S(1)}, s16[272,128]{1,0:T(8,128)(2,1)S(1)}) custom-call(s32[48]{0:T(128)S(1)} %copy-done.1, bf16[6,128,128]{2,1,0:T(8,128)(2,1)S(1)} %bitcast.21, bf16[6,128,128]{2,1,0:T(8,128)(2,1)S(1)} %collective-permute-done.refs_1_, bf16[3,128,128]{2,1,0:T(8,128)(2,1)S(1)} %get-tuple-element.24.refs_2_, ...), custom_call_target="tpu_custom_call" | custom-call | flops 100000000 | bytes 393216 | tf_op jit(solution)/shard_map/pallas_call | solution.py:115
  19.8 0.1 collective-permute-start.10
  19.9 1.0 %collective-permute-start.11 = (s16[272,128]{1,0:T(8,128)(2,1)S(1)}, s16[272,128]{1,0:T(8,128)(2,1)S(1)}, u32[]{:S(2)}, u32[]{:S(2)}) collective-permute-start(s16[272,128]{1,0:T(8,128)(2,1)S(1)} %get-tuple-element.19), channel_id=1, source_target_pairs={{0,3},{1,2},{2,1},{3,0},{4,7},{5,6},{6,5},{7,4},{8,11},{9,10},{10,... | collective-permute-start | bytes 208904 | tf_op jit(solution)/shard_map/ppermute | solution.py:161
  20.9 0.8 %shard_map.47.refs_10_ = f32[256,128]{1,0:T(8,128)S(1)} custom-call(s32[48]{0:T(128)S(1)} %copy-done.1, bf16[6,128,128]{2,1,0:T(8,128)(2,1)S(1)} %bitcast.22, bf16[6,128,128]{2,1,0:T(8,128)(2,1)S(1)} %collective-permute-done.refs_1_, bf16[3,128,128]{2,1,0:T(8,128)(2,1)S(1)} %get-tuple-element.24.refs_2_, ...), custom_call_target="tpu_custom_call" | custom-call | flops 100000000 | bytes 393216 | tf_op jit(solution)/shard_map/pallas_call | solution.py:115
  21.8 0.0 collective-permute-done.2.refs_0_
  21.8 1.8 %collective-permute-done.3.refs_1_ = bf16[6,128,128]{2,1,0:T(8,128)(2,1)S(1)} collective-permute-done((bf16[6,128,128]{2,1,0:T(8,128)(2,1)S(1)}, bf16[6,128,128]{2,1,0:T(8,128)(2,1)S(1)}, u32[]{:S(2)}, u32[]{:S(2)}) %collective-permute-start.3) | collective-permute-done | bytes 196640 | tf_op jit(solution)/shard_map/ppermute | solution.py:161
  23.6 0.9 %shard_map.48 = f32[256,128]{1,0:T(8,128)S(1)} custom-call(s32[48]{0:T(128)S(1)} %copy-done.1, bf16[6,128,128]{2,1,0:T(8,128)(2,1)S(1)} %collective-permute-done.2.refs_0_, bf16[6,128,128]{2,1,0:T(8,128)(2,1)S(1)} %collective-permute-done.3.refs_1_, bf16[3,128,128]{2,1,0:T(8,128)(2,1)S(1)} %get-tuple-element.24.refs_2_, ...), custom_call_target="tpu_custom_call" | custom-call | flops 99999997952 | bytes 393216 | tf_op jit(solution)/shard_map/pallas_call | solution.py:115
  24.5 1.5 %collective-permute-done.10 = s16[272,128]{1,0:T(8,128)(2,1)S(1)} collective-permute-done((s16[272,128]{1,0:T(8,128)(2,1)S(1)}, s16[272,128]{1,0:T(8,128)(2,1)S(1)}, u32[]{:S(2)}, u32[]{:S(2)}) %collective-permute-start.10) | collective-permute-done | bytes 69664 | tf_op jit(solution)/shard_map/ppermute | solution.py:161
  26.0 0.0 collective-permute-done.11
  26.0 0.7 %fusion.1 = bf16[256,128]{1,0:T(8,128)(2,1)} fusion(f32[256,128]{1,0:T(8,128)S(1)} %shard_map.48, f32[2,128]{1,0:T(2,128)S(1)} %get-tuple-element.25, s16[272,128]{1,0:T(8,128)(2,1)S(1)} %collective-permute-done.11, f32[2,128]{1,0:T(2,128)S(1)} %get-tuple-element.26, s16[272,128]{1,0:T(8,128)(2,1)S(1)} %collective-permute-done.10), kind=kLoop, calls=%fused_computation.2 | loop fusion | flops 229376 | bytes 329728 | tf_op jit(solution)/shard_map/convert_element_type | solution.py:223
  (1 shorter events, 0.0 us)
Async XLA Ops:
  0.0 13.5 %collective-permute-start = (bf16[6,128,128]{2,1,0:T(8,128)(2,1)}, bf16[6,128,128]{2,1,0:T(8,128)(2,1)S(1)}, u32[]{:S(2)}, u32[]{:S(2)}) collective-permute-start(bf16[6,128,128]{2,1,0:T(8,128)(2,1)} %bitcast.19), channel_id=1, source_target_pairs={{0,4},{1,5},{2,6},{3,7},{4,0},{5,1},{6,2},{7,3},{8,12},{9,13},{10,... | collective-permute-start | bytes 589832 | tf_op jit(solution)/shard_map/ppermute | solution.py:161
  4.0 8.0 %copy-start = (bf16[1,1,6,128,128]{4,3,2,1,0:T(8,128)(2,1)S(1)}, bf16[1,1,6,128,128]{4,3,2,1,0:T(8,128)(2,1)}, u32[]{:S(2)}) copy-start(bf16[1,1,6,128,128]{4,3,2,1,0:T(8,128)(2,1)} %param.4) | copy-start | bytes 589828
  5.0 7.0 %collective-permute-start.1 = (bf16[3,128,128]{2,1,0:T(8,128)(2,1)S(1)}, bf16[3,128,128]{2,1,0:T(8,128)(2,1)S(1)}, u32[]{:S(2)}, u32[]{:S(2)}) collective-permute-start(bf16[3,128,128]{2,1,0:T(8,128)(2,1)S(1)} %get-tuple-element.24.refs_2_), channel_id=1, source_target_pairs={{0,16},{8,24},{16,0},{24,8},{1,17},{9,25},{17,1},{25,9},{2,18},{10... | collective-permute-start | bytes 294920 | tf_op jit(solution)/shard_map/ppermute | solution.py:161
  6.6 7.6 %collective-permute-start.4 = (bf16[3,128,128]{2,1,0:T(8,128)(2,1)S(1)}, bf16[3,128,128]{2,1,0:T(8,128)(2,1)S(1)}, u32[]{:S(2)}, u32[]{:S(2)}) collective-permute-start(bf16[3,128,128]{2,1,0:T(8,128)(2,1)S(1)} %get-tuple-element.23), channel_id=1, source_target_pairs={{1,0},{0,1},{9,2},{8,3},{5,4},{4,5},{13,6},{12,7},{3,8},{2,9},{11,... | collective-permute-start | bytes 294920 | tf_op jit(solution)/shard_map/ppermute | solution.py:171
  8.1 6.9 %collective-permute-start.5 = (bf16[3,128,128]{2,1,0:T(8,128)(2,1)S(1)}, bf16[3,128,128]{2,1,0:T(8,128)(2,1)S(1)}, u32[]{:S(2)}, u32[]{:S(2)}) collective-permute-start(bf16[3,128,128]{2,1,0:T(8,128)(2,1)S(1)} %get-tuple-element.24.refs_2_), channel_id=1, source_target_pairs={{0,8},{8,0},{16,24},{24,16},{1,9},{9,1},{17,25},{25,17},{2,10},{10... | collective-permute-start | bytes 294920 | tf_op jit(solution)/shard_map/ppermute | solution.py:161
  9.2 5.9 %collective-permute-start.7 = (bf16[3,128,128]{2,1,0:T(8,128)(2,1)S(1)}, bf16[3,128,128]{2,1,0:T(8,128)(2,1)S(1)}, u32[]{:S(2)}, u32[]{:S(2)}) collective-permute-start(bf16[3,128,128]{2,1,0:T(8,128)(2,1)S(1)} %get-tuple-element.23), channel_id=1, source_target_pairs={{17,0},{16,1},{25,2},{24,3},{21,4},{20,5},{29,6},{28,7},{19,8},{18... | collective-permute-start | bytes 294920 | tf_op jit(solution)/shard_map/ppermute | solution.py:171
  12.1 9.7 %collective-permute-start.2 = (bf16[6,128,128]{2,1,0:T(8,128)(2,1)S(1)}, bf16[6,128,128]{2,1,0:T(8,128)(2,1)S(1)}, u32[]{:S(2)}, u32[]{:S(2)}) collective-permute-start(bf16[6,128,128]{2,1,0:T(8,128)(2,1)S(1)} %bitcast.20), channel_id=1, source_target_pairs={{0,2},{1,3},{2,0},{3,1},{4,6},{5,7},{6,4},{7,5},{8,10},{9,11},{10,... | collective-permute-start | bytes 589832 | tf_op jit(solution)/shard_map/ppermute | solution.py:161
  13.5 10.1 %collective-permute-start.3 = (bf16[6,128,128]{2,1,0:T(8,128)(2,1)S(1)}, bf16[6,128,128]{2,1,0:T(8,128)(2,1)S(1)}, u32[]{:S(2)}, u32[]{:S(2)}) collective-permute-start(bf16[6,128,128]{2,1,0:T(8,128)(2,1)S(1)} %collective-permute-done.refs_1_), channel_id=1, source_target_pairs={{0,2},{1,3},{2,0},{3,1},{4,6},{5,7},{6,4},{7,5},{8,10},{9,11},{10,... | collective-permute-start | bytes 589832 | tf_op jit(solution)/shard_map/ppermute | solution.py:161
  14.2 2.7 %collective-permute-start.8 = (bf16[3,128,128]{2,1,0:T(8,128)(2,1)S(1)}, bf16[3,128,128]{2,1,0:T(8,128)(2,1)S(1)}, u32[]{:S(2)}, u32[]{:S(2)}) collective-permute-start(bf16[3,128,128]{2,1,0:T(8,128)(2,1)S(1)} %collective-permute-done.1.refs_6_), channel_id=1, source_target_pairs={{0,8},{8,0},{16,24},{24,16},{1,9},{9,1},{17,25},{25,17},{2,10},{10... | collective-permute-start | bytes 294920 | tf_op jit(solution)/shard_map/ppermute | solution.py:161
  15.0 1.9 %collective-permute-start.6 = (bf16[3,128,128]{2,1,0:T(8,128)(2,1)S(1)}, bf16[3,128,128]{2,1,0:T(8,128)(2,1)S(1)}, u32[]{:S(2)}, u32[]{:S(2)}) collective-permute-start(bf16[3,128,128]{2,1,0:T(8,128)(2,1)S(1)} %collective-permute-done.4.refs_3_), channel_id=1, source_target_pairs={{0,8},{8,0},{16,24},{24,16},{1,9},{9,1},{17,25},{25,17},{2,10},{10... | collective-permute-start | bytes 294920 | tf_op jit(solution)/shard_map/ppermute | solution.py:161
  15.1 2.8 %collective-permute-start.9 = (bf16[3,128,128]{2,1,0:T(8,128)(2,1)S(1)}, bf16[3,128,128]{2,1,0:T(8,128)(2,1)S(1)}, u32[]{:S(2)}, u32[]{:S(2)}) collective-permute-start(bf16[3,128,128]{2,1,0:T(8,128)(2,1)S(1)} %collective-permute-done.7.refs_7_), channel_id=1, source_target_pairs={{0,8},{8,0},{16,24},{24,16},{1,9},{9,1},{17,25},{25,17},{2,10},{10... | collective-permute-start | bytes 294920 | tf_op jit(solution)/shard_map/ppermute | solution.py:161
  17.9 0.7 %copy-start.1 = (s32[48]{0:T(128)S(1)}, s32[48]{0:T(128)}, u32[]{:S(2)}) copy-start(s32[48]{0:T(128)} %shard_map.46.codes_ref) | copy-start | bytes 580
  19.8 6.2 %collective-permute-start.10 = (s16[272,128]{1,0:T(8,128)(2,1)S(1)}, s16[272,128]{1,0:T(8,128)(2,1)S(1)}, u32[]{:S(2)}, u32[]{:S(2)}) collective-permute-start(s16[272,128]{1,0:T(8,128)(2,1)S(1)} %get-tuple-element.18), channel_id=1, source_target_pairs={{0,1},{1,0},{2,3},{3,2},{4,5},{5,4},{6,7},{7,6},{8,9},{9,8},{10,11... | collective-permute-start | bytes 208904 | tf_op jit(solution)/shard_map/ppermute | solution.py:161
  19.9 6.1 %collective-permute-start.11 = (s16[272,128]{1,0:T(8,128)(2,1)S(1)}, s16[272,128]{1,0:T(8,128)(2,1)S(1)}, u32[]{:S(2)}, u32[]{:S(2)}) collective-permute-start(s16[272,128]{1,0:T(8,128)(2,1)S(1)} %get-tuple-element.19), channel_id=1, source_target_pairs={{0,3},{1,2},{2,1},{3,0},{4,7},{5,6},{6,5},{7,4},{8,11},{9,10},{10,... | collective-permute-start | bytes 208904 | tf_op jit(solution)/shard_map/ppermute | solution.py:161

commit v4 on v3

--- a/solution.py
+++ b/solution.py
@@ -199,12 +199,13 @@
     right = right_tiles[0, 0]
     tile = left.shape[-1]
 
-    codes = find_matches(left_index, right_index)
     given = lax.dynamic_index_in_dim(right, 1 - y, 0, keepdims=False)
     own = lax.dynamic_index_in_dim(right, y, 0, keepdims=False)
     pairs = []
     for t in range(0, lax.axis_size("row"), 2):
         pairs.append([across(own, "row", t) if t else own, other_half(given, t)])
+    left_index, pairs[-1][0] = lax.optimization_barrier((left_index, pairs[-1][0]))
+    codes = find_matches(left_index, right_index)
     lefts, codes, pairs[-1][0] = gather(left, codes, pairs[-1][0])
     rights = []
     for pair in pairs:

time: 27 us -> 27.4 us (1.015)
  waiting for transfers between devices: 4.63 us -> 5.07 us
    ppermute x10, waiting for transfers between devices: 4.52 us -> 5.07 us  [across(): return lax.ppermute(block, axis, route)]
  transfers between devices with their start and end apart: 12 -> 12, of which waited for: 5 -> 5; matrix products, arithmetic and copies ran while one was open for 4% -> 4% of each run, Pallas kernels for 20% -> 19%
where the time goes in v4:
time: 27.4 us; the launch traced here: 27.1 us
  starting transfers between devices  14.4 us (53%)
  Pallas kernels  5.18 us (19%)
  waiting for transfers between devices  5.07 us (19%)
  local copies, waits for them, and re-layouts  1.65 us (6%)
  other arithmetic  0.71 us (3%)
    ppermute x10, starting transfers between devices, across(): return lax.ppermute(block, axis, route)  12.4 us
    ppermute x10, waiting for transfers between devices, across(): return lax.ppermute(block, axis, route)  5.07 us
    pallas_call x3, Pallas kernels, products(): pl.pallas_call(kernel, out_shape=[out_shape] * len(sides), in_specs=[SMEM...  2.88 us
    pallas_call x1, Pallas kernels, find_matches(): pl.pallas_call(kernel, out_shape=jax.ShapeDtypeStruct((total,), jnp.int32...  2.3 us
    ppermute x2, starting transfers between devices, travel(): return lax.ppermute(block, ('row', 'col'), route)  2 us
    squeeze x1, local copies, waits for them, and re-layouts, shards(): given = lax.dynamic_index_in_dim(right, 1 - y, 0, keepdims=False)  0.99 us
    convert_element_type x1, other arithmetic, shards(): return (mine + decoded(coming) + decoded(from_far)).astype(jnp.bfloat16)  0.69 us
    unnamed x4, local copies, waits for them, and re-layouts  0.66 us
  transfers between devices with their start and end apart: 12, of which 5 were waited for; matrix products, arithmetic and copies ran while one was open for 4% of the time, Pallas kernels for 19%

profile of v4, /device:TPU:0, one launch (start us, length us, event | category | flops | bytes accessed | tf_op | source)
XLA Modules:
  0.0 27.1 jit_solution(12526120991280575440)
XLA Ops:
  0.0 4.0 %collective-permute-start = (bf16[6,128,128]{2,1,0:T(8,128)(2,1)}, bf16[6,128,128]{2,1,0:T(8,128)(2,1)S(1)}, u32[]{:S(2)}, u32[]{:S(2)}) collective-permute-start(bf16[6,128,128]{2,1,0:T(8,128)(2,1)} %bitcast.19), channel_id=1, source_target_pairs={{0,4},{1,5},{2,6},{3,7},{4,0},{5,1},{6,2},{7,3},{8,12},{9,13},{10,... | collective-permute-start | bytes 589832 | tf_op jit(solution)/shard_map/ppermute | solution.py:161
  4.0 0.0 copy-start
  4.0 1.0 %dynamic-slice_bitcast_fusion = (bf16[3,128,128]{2,1,0:T(8,128)(2,1)S(1)}, bf16[3,128,128]{2,1,0:T(8,128)(2,1)S(1)}) fusion(bf16[1,1,2,3,128,128]{5,4,3,2,1,0:T(8,128)(2,1)} %param.6, s32[]{:T(128)S(6)} %select_n.8, s32[]{:T(128)S(6)} %select_n.7), kind=kLoop, calls=%fused_computation.5 | loop fusion | bytes 393224 | tf_op jit(solution)/shard_map/jit(dynamic_index_in_dim)/squeeze | solution.py:202
  5.0 1.6 %collective-permute-start.1 = (bf16[3,128,128]{2,1,0:T(8,128)(2,1)S(1)}, bf16[3,128,128]{2,1,0:T(8,128)(2,1)S(1)}, u32[]{:S(2)}, u32[]{:S(2)}) collective-permute-start(bf16[3,128,128]{2,1,0:T(8,128)(2,1)S(1)} %get-tuple-element.28.refs_2_), channel_id=1, source_target_pairs={{0,16},{8,24},{16,0},{24,8},{1,17},{9,25},{17,1},{25,9},{2,18},{10... | collective-permute-start | bytes 294920 | tf_op jit(solution)/shard_map/ppermute | solution.py:161
  6.6 1.5 %collective-permute-start.4 = (bf16[3,128,128]{2,1,0:T(8,128)(2,1)S(1)}, bf16[3,128,128]{2,1,0:T(8,128)(2,1)S(1)}, u32[]{:S(2)}, u32[]{:S(2)}) collective-permute-start(bf16[3,128,128]{2,1,0:T(8,128)(2,1)S(1)} %get-tuple-element.27), channel_id=1, source_target_pairs={{1,0},{0,1},{9,2},{8,3},{5,4},{4,5},{13,6},{12,7},{3,8},{2,9},{11,... | collective-permute-start | bytes 294920 | tf_op jit(solution)/shard_map/ppermute | solution.py:171
  8.1 0.5 %collective-permute-start.7 = (bf16[3,128,128]{2,1,0:T(8,128)(2,1)S(1)}, bf16[3,128,128]{2,1,0:T(8,128)(2,1)S(1)}, u32[]{:S(2)}, u32[]{:S(2)}) collective-permute-start(bf16[3,128,128]{2,1,0:T(8,128)(2,1)S(1)} %get-tuple-element.27), channel_id=1, source_target_pairs={{17,0},{16,1},{25,2},{24,3},{21,4},{20,5},{29,6},{28,7},{19,8},{18... | collective-permute-start | bytes 294920 | tf_op jit(solution)/shard_map/ppermute | solution.py:171
  8.6 0.7 %collective-permute-start.5 = (bf16[3,128,128]{2,1,0:T(8,128)(2,1)S(1)}, bf16[3,128,128]{2,1,0:T(8,128)(2,1)S(1)}, u32[]{:S(2)}, u32[]{:S(2)}) collective-permute-start(bf16[3,128,128]{2,1,0:T(8,128)(2,1)S(1)} %get-tuple-element.28.refs_2_), channel_id=1, source_target_pairs={{0,8},{8,0},{16,24},{24,16},{1,9},{9,1},{17,25},{25,17},{2,10},{10... | collective-permute-start | bytes 294920 | tf_op jit(solution)/shard_map/ppermute | solution.py:161
  9.2 0.5 %collective-permute-done.1.refs_6_ = bf16[3,128,128]{2,1,0:T(8,128)(2,1)S(1)} collective-permute-done((bf16[3,128,128]{2,1,0:T(8,128)(2,1)S(1)}, bf16[3,128,128]{2,1,0:T(8,128)(2,1)S(1)}, u32[]{:S(2)}, u32[]{:S(2)}) %collective-permute-start.1) | collective-permute-done | bytes 98336 | tf_op jit(solution)/shard_map/ppermute | solution.py:161
  9.7 0.0 copy-done
  9.7 1.7 %collective-permute-start.2 = (bf16[6,128,128]{2,1,0:T(8,128)(2,1)S(1)}, bf16[6,128,128]{2,1,0:T(8,128)(2,1)S(1)}, u32[]{:S(2)}, u32[]{:S(2)}) collective-permute-start(bf16[6,128,128]{2,1,0:T(8,128)(2,1)S(1)} %bitcast.20), channel_id=1, source_target_pairs={{0,2},{1,3},{2,0},{3,1},{4,6},{5,7},{6,4},{7,5},{8,10},{9,11},{10,... | collective-permute-start | bytes 589832 | tf_op jit(solution)/shard_map/ppermute | solution.py:161
  11.4 2.3 %shard_map.46.codes_ref = s32[48]{0:T(128)} custom-call(s32[6,4,8]{2,1,0:T(4,128)} %bitcast.23, s32[4,3,2,8]{3,2,1,0:T(2,128)} %bitcast.24), custom_call_target="tpu_custom_call" | custom-call | tf_op jit(solution)/shard_map/pallas_call | solution.py:60
  13.7 0.0 collective-permute-done.refs_1_
  13.7 0.5 %collective-permute-start.3 = (bf16[6,128,128]{2,1,0:T(8,128)(2,1)S(1)}, bf16[6,128,128]{2,1,0:T(8,128)(2,1)S(1)}, u32[]{:S(2)}, u32[]{:S(2)}) collective-permute-start(bf16[6,128,128]{2,1,0:T(8,128)(2,1)S(1)} %collective-permute-done.refs_1_), channel_id=1, source_target_pairs={{0,2},{1,3},{2,0},{3,1},{4,6},{5,7},{6,4},{7,5},{8,10},{9,11},{10,... | collective-permute-start | bytes 589832 | tf_op jit(solution)/shard_map/ppermute | solution.py:161
  14.2 0.0 collective-permute-done.4.refs_3_
  14.2 0.7 %collective-permute-start.8 = (bf16[3,128,128]{2,1,0:T(8,128)(2,1)S(1)}, bf16[3,128,128]{2,1,0:T(8,128)(2,1)S(1)}, u32[]{:S(2)}, u32[]{:S(2)}) collective-permute-start(bf16[3,128,128]{2,1,0:T(8,128)(2,1)S(1)} %collective-permute-done.1.refs_6_), channel_id=1, source_target_pairs={{0,8},{8,0},{16,24},{24,16},{1,9},{9,1},{17,25},{25,17},{2,10},{10... | collective-permute-start | bytes 294920 | tf_op jit(solution)/shard_map/ppermute | solution.py:161
  14.9 0.0 collective-permute-done.7.refs_7_
  14.9 2.3 %collective-permute-start.6 = (bf16[3,128,128]{2,1,0:T(8,128)(2,1)S(1)}, bf16[3,128,128]{2,1,0:T(8,128)(2,1)S(1)}, u32[]{:S(2)}, u32[]{:S(2)}) collective-permute-start(bf16[3,128,128]{2,1,0:T(8,128)(2,1)S(1)} %collective-permute-done.4.refs_3_), channel_id=1, source_target_pairs={{0,8},{8,0},{16,24},{24,16},{1,9},{9,1},{17,25},{25,17},{2,10},{10... | collective-permute-start | bytes 294920 | tf_op jit(solution)/shard_map/ppermute | solution.py:161
  17.2 0.0 collective-permute-done.5.refs_4_
  17.2 0.0 collective-permute-start.9
  17.2 0.0 collective-permute-done.8.refs_8_
  17.2 0.9 %collective-permute-done.6.refs_5_ = bf16[3,128,128]{2,1,0:T(8,128)(2,1)S(1)} collective-permute-done((bf16[3,128,128]{2,1,0:T(8,128)(2,1)S(1)}, bf16[3,128,128]{2,1,0:T(8,128)(2,1)S(1)}, u32[]{:S(2)}, u32[]{:S(2)}) %collective-permute-start.6) | collective-permute-done | bytes 98336 | tf_op jit(solution)/shard_map/ppermute | solution.py:161
  18.2 0.4 %collective-permute-done.9.refs_9_ = bf16[3,128,128]{2,1,0:T(8,128)(2,1)S(1)} collective-permute-done((bf16[3,128,128]{2,1,0:T(8,128)(2,1)S(1)}, bf16[3,128,128]{2,1,0:T(8,128)(2,1)S(1)}, u32[]{:S(2)}, u32[]{:S(2)}) %collective-permute-start.9) | collective-permute-done | bytes 98336 | tf_op jit(solution)/shard_map/ppermute | solution.py:161
  18.5 0.0 copy-start.1
  18.5 0.7 %copy-done.1 = s32[48]{0:T(128)S(1)} copy-done((s32[48]{0:T(128)S(1)}, s32[48]{0:T(128)}, u32[]{:S(2)}) %copy-start.1) | copy-done | bytes 216
  19.2 1.1 %shard_map.49 = (s16[272,128]{1,0:T(8,128)(2,1)S(1)}, s16[272,128]{1,0:T(8,128)(2,1)S(1)}) custom-call(s32[48]{0:T(128)S(1)} %copy-done.1, bf16[6,128,128]{2,1,0:T(8,128)(2,1)S(1)} %bitcast.21, bf16[6,128,128]{2,1,0:T(8,128)(2,1)S(1)} %collective-permute-done.refs_1_, bf16[3,128,128]{2,1,0:T(8,128)(2,1)S(1)} %get-tuple-element.28.refs_2_, ...), custom_call_target="tpu_custom_call" | custom-call | flops 100000000 | bytes 393216 | tf_op jit(solution)/shard_map/pallas_call | solution.py:115
  20.3 0.6 %collective-permute-start.10 = (s16[272,128]{1,0:T(8,128)(2,1)S(1)}, s16[272,128]{1,0:T(8,128)(2,1)S(1)}, u32[]{:S(2)}, u32[]{:S(2)}) collective-permute-start(s16[272,128]{1,0:T(8,128)(2,1)S(1)} %get-tuple-element.22), channel_id=1, source_target_pairs={{0,1},{1,0},{2,3},{3,2},{4,5},{5,4},{6,7},{7,6},{8,9},{9,8},{10,11... | collective-permute-start | bytes 208904 | tf_op jit(solution)/shard_map/ppermute | solution.py:161
  20.9 0.3 %collective-permute-start.11 = (s16[272,128]{1,0:T(8,128)(2,1)S(1)}, s16[272,128]{1,0:T(8,128)(2,1)S(1)}, u32[]{:S(2)}, u32[]{:S(2)}) collective-permute-start(s16[272,128]{1,0:T(8,128)(2,1)S(1)} %get-tuple-element.23), channel_id=1, source_target_pairs={{0,3},{1,2},{2,1},{3,0},{4,7},{5,6},{6,5},{7,4},{8,11},{9,10},{10,... | collective-permute-start | bytes 208904 | tf_op jit(solution)/shard_map/ppermute | solution.py:161
  21.3 0.9 %shard_map.47.refs_10_ = f32[256,128]{1,0:T(8,128)S(1)} custom-call(s32[48]{0:T(128)S(1)} %copy-done.1, bf16[6,128,128]{2,1,0:T(8,128)(2,1)S(1)} %bitcast.22, bf16[6,128,128]{2,1,0:T(8,128)(2,1)S(1)} %collective-permute-done.refs_1_, bf16[3,128,128]{2,1,0:T(8,128)(2,1)S(1)} %get-tuple-element.28.refs_2_, ...), custom_call_target="tpu_custom_call" | custom-call | flops 100000000 | bytes 393216 | tf_op jit(solution)/shard_map/pallas_call | solution.py:115
  22.2 0.0 collective-permute-done.2.refs_0_
  22.2 1.4 %collective-permute-done.3.refs_1_ = bf16[6,128,128]{2,1,0:T(8,128)(2,1)S(1)} collective-permute-done((bf16[6,128,128]{2,1,0:T(8,128)(2,1)S(1)}, bf16[6,128,128]{2,1,0:T(8,128)(2,1)S(1)}, u32[]{:S(2)}, u32[]{:S(2)}) %collective-permute-start.3) | collective-permute-done | bytes 196640 | tf_op jit(solution)/shard_map/ppermute | solution.py:161
  23.6 0.9 %shard_map.48 = f32[256,128]{1,0:T(8,128)S(1)} custom-call(s32[48]{0:T(128)S(1)} %copy-done.1, bf16[6,128,128]{2,1,0:T(8,128)(2,1)S(1)} %collective-permute-done.2.refs_0_, bf16[6,128,128]{2,1,0:T(8,128)(2,1)S(1)} %collective-permute-done.3.refs_1_, bf16[3,128,128]{2,1,0:T(8,128)(2,1)S(1)} %get-tuple-element.28.refs_2_, ...), custom_call_target="tpu_custom_call" | custom-call | flops 99999997952 | bytes 393216 | tf_op jit(solution)/shard_map/pallas_call | solution.py:115
  24.5 1.9 %collective-permute-done.10 = s16[272,128]{1,0:T(8,128)(2,1)S(1)} collective-permute-done((s16[272,128]{1,0:T(8,128)(2,1)S(1)}, s16[272,128]{1,0:T(8,128)(2,1)S(1)}, u32[]{:S(2)}, u32[]{:S(2)}) %collective-permute-start.10) | collective-permute-done | bytes 69664 | tf_op jit(solution)/shard_map/ppermute | solution.py:161
  26.4 0.0 collective-permute-done.11
  26.4 0.7 %fusion.1 = bf16[256,128]{1,0:T(8,128)(2,1)} fusion(f32[256,128]{1,0:T(8,128)S(1)} %shard_map.48, f32[2,128]{1,0:T(2,128)S(1)} %get-tuple-element.29, s16[272,128]{1,0:T(8,128)(2,1)S(1)} %collective-permute-done.11, f32[2,128]{1,0:T(2,128)S(1)} %get-tuple-element.30, s16[272,128]{1,0:T(8,128)(2,1)S(1)} %collective-permute-done.10), kind=kLoop, calls=%fused_computation.2 | loop fusion | flops 229376 | bytes 329728 | tf_op jit(solution)/shard_map/convert_element_type | solution.py:224
  (1 shorter events, 0.0 us)
Async XLA Ops:
  0.0 13.7 %collective-permute-start = (bf16[6,128,128]{2,1,0:T(8,128)(2,1)}, bf16[6,128,128]{2,1,0:T(8,128)(2,1)S(1)}, u32[]{:S(2)}, u32[]{:S(2)}) collective-permute-start(bf16[6,128,128]{2,1,0:T(8,128)(2,1)} %bitcast.19), channel_id=1, source_target_pairs={{0,4},{1,5},{2,6},{3,7},{4,0},{5,1},{6,2},{7,3},{8,12},{9,13},{10,... | collective-permute-start | bytes 589832 | tf_op jit(solution)/shard_map/ppermute | solution.py:161
  4.0 5.7 %copy-start = (bf16[1,1,6,128,128]{4,3,2,1,0:T(8,128)(2,1)S(1)}, bf16[1,1,6,128,128]{4,3,2,1,0:T(8,128)(2,1)}, u32[]{:S(2)}) copy-start(bf16[1,1,6,128,128]{4,3,2,1,0:T(8,128)(2,1)} %param.4) | copy-start | bytes 589828
  5.0 4.7 %collective-permute-start.1 = (bf16[3,128,128]{2,1,0:T(8,128)(2,1)S(1)}, bf16[3,128,128]{2,1,0:T(8,128)(2,1)S(1)}, u32[]{:S(2)}, u32[]{:S(2)}) collective-permute-start(bf16[3,128,128]{2,1,0:T(8,128)(2,1)S(1)} %get-tuple-element.28.refs_2_), channel_id=1, source_target_pairs={{0,16},{8,24},{16,0},{24,8},{1,17},{9,25},{17,1},{25,9},{2,18},{10... | collective-permute-start | bytes 294920 | tf_op jit(solution)/shard_map/ppermute | solution.py:161
  6.6 7.6 %collective-permute-start.4 = (bf16[3,128,128]{2,1,0:T(8,128)(2,1)S(1)}, bf16[3,128,128]{2,1,0:T(8,128)(2,1)S(1)}, u32[]{:S(2)}, u32[]{:S(2)}) collective-permute-start(bf16[3,128,128]{2,1,0:T(8,128)(2,1)S(1)} %get-tuple-element.27), channel_id=1, source_target_pairs={{1,0},{0,1},{9,2},{8,3},{5,4},{4,5},{13,6},{12,7},{3,8},{2,9},{11,... | collective-permute-start | bytes 294920 | tf_op jit(solution)/shard_map/ppermute | solution.py:171
  8.1 6.8 %collective-permute-start.7 = (bf16[3,128,128]{2,1,0:T(8,128)(2,1)S(1)}, bf16[3,128,128]{2,1,0:T(8,128)(2,1)S(1)}, u32[]{:S(2)}, u32[]{:S(2)}) collective-permute-start(bf16[3,128,128]{2,1,0:T(8,128)(2,1)S(1)} %get-tuple-element.27), channel_id=1, source_target_pairs={{17,0},{16,1},{25,2},{24,3},{21,4},{20,5},{29,6},{28,7},{19,8},{18... | collective-permute-start | bytes 294920 | tf_op jit(solution)/shard_map/ppermute | solution.py:171
  8.6 8.6 %collective-permute-start.5 = (bf16[3,128,128]{2,1,0:T(8,128)(2,1)S(1)}, bf16[3,128,128]{2,1,0:T(8,128)(2,1)S(1)}, u32[]{:S(2)}, u32[]{:S(2)}) collective-permute-start(bf16[3,128,128]{2,1,0:T(8,128)(2,1)S(1)} %get-tuple-element.28.refs_2_), channel_id=1, source_target_pairs={{0,8},{8,0},{16,24},{24,16},{1,9},{9,1},{17,25},{25,17},{2,10},{10... | collective-permute-start | bytes 294920 | tf_op jit(solution)/shard_map/ppermute | solution.py:161
  9.7 12.4 %collective-permute-start.2 = (bf16[6,128,128]{2,1,0:T(8,128)(2,1)S(1)}, bf16[6,128,128]{2,1,0:T(8,128)(2,1)S(1)}, u32[]{:S(2)}, u32[]{:S(2)}) collective-permute-start(bf16[6,128,128]{2,1,0:T(8,128)(2,1)S(1)} %bitcast.20), channel_id=1, source_target_pairs={{0,2},{1,3},{2,0},{3,1},{4,6},{5,7},{6,4},{7,5},{8,10},{9,11},{10,... | collective-permute-start | bytes 589832 | tf_op jit(solution)/shard_map/ppermute | solution.py:161
  13.7 9.9 %collective-permute-start.3 = (bf16[6,128,128]{2,1,0:T(8,128)(2,1)S(1)}, bf16[6,128,128]{2,1,0:T(8,128)(2,1)S(1)}, u32[]{:S(2)}, u32[]{:S(2)}) collective-permute-start(bf16[6,128,128]{2,1,0:T(8,128)(2,1)S(1)} %collective-permute-done.refs_1_), channel_id=1, source_target_pairs={{0,2},{1,3},{2,0},{3,1},{4,6},{5,7},{6,4},{7,5},{8,10},{9,11},{10,... | collective-permute-start | bytes 589832 | tf_op jit(solution)/shard_map/ppermute | solution.py:161
  14.2 3.0 %collective-permute-start.8 = (bf16[3,128,128]{2,1,0:T(8,128)(2,1)S(1)}, bf16[3,128,128]{2,1,0:T(8,128)(2,1)S(1)}, u32[]{:S(2)}, u32[]{:S(2)}) collective-permute-start(bf16[3,128,128]{2,1,0:T(8,128)(2,1)S(1)} %collective-permute-done.1.refs_6_), channel_id=1, source_target_pairs={{0,8},{8,0},{16,24},{24,16},{1,9},{9,1},{17,25},{25,17},{2,10},{10... | collective-permute-start | bytes 294920 | tf_op jit(solution)/shard_map/ppermute | solution.py:161
  14.9 3.3 %collective-permute-start.6 = (bf16[3,128,128]{2,1,0:T(8,128)(2,1)S(1)}, bf16[3,128,128]{2,1,0:T(8,128)(2,1)S(1)}, u32[]{:S(2)}, u32[]{:S(2)}) collective-permute-start(bf16[3,128,128]{2,1,0:T(8,128)(2,1)S(1)} %collective-permute-done.4.refs_3_), channel_id=1, source_target_pairs={{0,8},{8,0},{16,24},{24,16},{1,9},{9,1},{17,25},{25,17},{2,10},{10... | collective-permute-start | bytes 294920 | tf_op jit(solution)/shard_map/ppermute | solution.py:161
  17.2 1.3 %collective-permute-start.9 = (bf16[3,128,128]{2,1,0:T(8,128)(2,1)S(1)}, bf16[3,128,128]{2,1,0:T(8,128)(2,1)S(1)}, u32[]{:S(2)}, u32[]{:S(2)}) collective-permute-start(bf16[3,128,128]{2,1,0:T(8,128)(2,1)S(1)} %collective-permute-done.7.refs_7_), channel_id=1, source_target_pairs={{0,8},{8,0},{16,24},{24,16},{1,9},{9,1},{17,25},{25,17},{2,10},{10... | collective-permute-start | bytes 294920 | tf_op jit(solution)/shard_map/ppermute | solution.py:161
  18.5 0.7 %copy-start.1 = (s32[48]{0:T(128)S(1)}, s32[48]{0:T(128)}, u32[]{:S(2)}) copy-start(s32[48]{0:T(128)} %shard_map.46.codes_ref) | copy-start | bytes 580
  20.3 6.1 %collective-permute-start.10 = (s16[272,128]{1,0:T(8,128)(2,1)S(1)}, s16[272,128]{1,0:T(8,128)(2,1)S(1)}, u32[]{:S(2)}, u32[]{:S(2)}) collective-permute-start(s16[272,128]{1,0:T(8,128)(2,1)S(1)} %get-tuple-element.22), channel_id=1, source_target_pairs={{0,1},{1,0},{2,3},{3,2},{4,5},{5,4},{6,7},{7,6},{8,9},{9,8},{10,11... | collective-permute-start | bytes 208904 | tf_op jit(solution)/shard_map/ppermute | solution.py:161
  20.9 5.5 %collective-permute-start.11 = (s16[272,128]{1,0:T(8,128)(2,1)S(1)}, s16[272,128]{1,0:T(8,128)(2,1)S(1)}, u32[]{:S(2)}, u32[]{:S(2)}) collective-permute-start(s16[272,128]{1,0:T(8,128)(2,1)S(1)} %get-tuple-element.23), channel_id=1, source_target_pairs={{0,3},{1,2},{2,1},{3,0},{4,7},{5,6},{6,5},{7,4},{8,11},{9,10},{10,... | collective-permute-start | bytes 208904 | tf_op jit(solution)/shard_map/ppermute | solution.py:161

commit v5 on v1

--- a/solution.py
+++ b/solution.py
@@ -8,6 +8,7 @@
 KT = 8
 RT = 2
 SIDES = 3
+HOLD = 12 * 10**8
 EARLY = 10**8
 LATE = 10**11
 BITS = 15
@@ -63,6 +64,7 @@
         out_shape=jax.ShapeDtypeStruct((total,), jnp.int32),
         in_specs=[SMEM] * 2,
         out_specs=SMEM,
+        compiler_params=pltpu.CompilerParams(vmem_limit_bytes=2 * 1024 * 1024),
     )(left_index, right_index)
 
 
@@ -131,8 +133,103 @@
     )(codes, *[lefts[s] for s in distances], *rights, *starts)
 
 
-def write_sum(sum_ref, out_ref):
-    out_ref[...] = sum_ref[...]
+def own_products(codes, early, late, rights, flops):
+    distances = sorted(early)
+    count = len(early)
+    places = len(rights) // 2
+    right_slots, tile, _ = rights[0].shape
+    slots = early[0].shape[0]
+
+    def kernel(codes_ref, *refs):
+        left_refs = dict(zip(distances, refs))
+        right_refs = refs[count : count + places]
+        total_ref, dense_ref, held = refs[count + places :]
+        row, z, _ = position()
+        for t in range(places):
+            held[t] = right_refs[t][...]
+        dense_ref[...] = jnp.zeros_like(dense_ref)
+        for n, s in enumerate(late):
+            base = code_at(s, 0, places, slots)
+            at = row ^ z ^ s
+
+            @pl.loop(0, slots)
+            def _(slot):
+                code = codes_ref[base + slot]
+
+                @pl.when(code > 0)
+                def _():
+                    rows = pl.ds(pl.multiple_of(slot * tile, tile), tile)
+                    i = lax.div(code - 1, right_slots)
+                    columns = pl.ds(pl.multiple_of(i * tile, tile), tile)
+                    dense_ref[n, rows, columns] = held[at, lax.rem(code - 1, right_slots)]
+
+        total_ref[...] = jnp.zeros_like(total_ref)
+        for s in distances:
+            at = row ^ z ^ s
+            add_block(
+                codes_ref, code_at(s, 0, places, slots), left_refs[s],
+                lambda found, at=at: held[at, found], right_slots, total_ref,
+            )
+
+    return pl.pallas_call(
+        kernel,
+        out_shape=[
+            jax.ShapeDtypeStruct((RT * tile, tile), jnp.float32),
+            jax.ShapeDtypeStruct((len(late), slots * tile, RT * tile), jnp.bfloat16),
+        ],
+        in_specs=[SMEM] + [VMEM] * (count + places),
+        out_specs=[VMEM] * 2,
+        scratch_shapes=[pltpu.VMEM((places, right_slots, tile, tile), jnp.bfloat16)],
+        compiler_params=pltpu.CompilerParams(vmem_limit_bytes=32 * 1024 * 1024),
+        cost_estimate=pl.CostEstimate(flops=flops, bytes_accessed=2 * slots * tile**2, transcendentals=0),
+    )(codes, *[early[s] for s in distances], *rights[::2])
+
+
+def last_products(lefts, dense, total, flops):
+    count = len(lefts)
+    slots, tile, _ = lefts[0].shape
+
+    def kernel(*refs):
+        left_refs = refs[:count]
+        dense_ref, total_ref, out_ref = refs[count:]
+        added = jnp.zeros((tile, RT * tile), jnp.float32)
+        for n, left_ref in enumerate(left_refs):
+            for slot in range(0, slots, 2):
+                both = min(2, slots - slot)
+                added += jnp.dot(
+                    jnp.concatenate([left_ref[slot + m] for m in range(both)], axis=1),
+                    dense_ref[n, slot * tile : (slot + both) * tile, :],
+                    preferred_element_type=jnp.float32,
+                )
+        for i in range(RT):
+            rows = slice(i * tile, (i + 1) * tile)
+            out_ref[rows, :] = total_ref[rows, :] + added[:, rows]
+
+    return pl.pallas_call(
+        kernel,
+        out_shape=jax.ShapeDtypeStruct(total.shape, total.dtype),
+        in_specs=[VMEM] * (count + 2),
+        out_specs=VMEM,
+        compiler_params=pltpu.CompilerParams(vmem_limit_bytes=16 * 1024 * 1024),
+        cost_estimate=pl.CostEstimate(flops=flops, bytes_accessed=2 * slots * tile**2, transcendentals=0),
+    )(*lefts, dense, total)
+
+
+def hold(blocks):
+    count = len(blocks)
+
+    def kernel(*refs):
+        for block_ref, out_ref in zip(refs[:count], refs[count:]):
+            out_ref[...] = block_ref[...]
+
+    return pl.pallas_call(
+        kernel,
+        out_shape=[jax.ShapeDtypeStruct(block.shape, block.dtype) for block in blocks],
+        in_specs=[VMEM] * count,
+        out_specs=[VMEM] * count,
+        compiler_params=pltpu.CompilerParams(vmem_limit_bytes=4 * 1024 * 1024),
+        cost_estimate=pl.CostEstimate(flops=HOLD, bytes_accessed=0, transcendentals=0),
+    )(*blocks)
 
 
 def write_coded(sum_ref, out_ref):
@@ -205,22 +302,23 @@
     given = lax.dynamic_index_in_dim(right, 1 - y, 0, keepdims=False)
     own = lax.dynamic_index_in_dim(right, y, 0, keepdims=False)
     lefts, codes, (own, given) = gather(left, codes, (own, given))
+    places = range(0, lax.axis_size("row"), 2)
+    others = hold([other_half(given, t) for t in places])
     rights = []
-    for t in range(0, lax.axis_size("row"), 2):
-        pair = [across(own, "row", t) if t else own, other_half(given, t)]
+    for t, other in zip(places, others):
+        pair = [across(own, "row", t) if t else own, other]
         if not t:
             pair[0], lefts[1] = lax.optimization_barrier((pair[0], lefts[1]))
         rights += pair + [across(half, "row", 1) for half in pair]
 
-    plain = jax.ShapeDtypeStruct((RT * tile, tile), jnp.float32)
     coded = jax.ShapeDtypeStruct((RT * tile + PAD, tile), jnp.int16)
     early = {s: lefts[s] for s in counting(1, len(lefts))}
-    late = {s: lefts[s] for s in lefts if s not in early}
+    late = [s for s in sorted(lefts) if s not in early]
     to_other, to_far = products(codes, early, rights, (1, 2), write_coded, coded, EARLY)
     coming = across(to_other, "col", 1)
     from_far = across(to_far, "col", 3)
-    (mine,) = products(codes, early, rights, (0,), write_sum, plain, 10**8)
-    (mine,) = products(codes, late, rights, (0,), write_sum, plain, LATE, mine)
+    mine, dense = own_products(codes, early, late, rights, 10**8)
+    mine = last_products([lefts[s] for s in late], dense, mine, LATE)
     mine, coming, from_far = lax.optimization_barrier((mine, coming, from_far))
     return (mine + decoded(coming) + decoded(from_far)).astype(jnp.bfloat16)
 

time: 28.3 us -> 27.9 us (0.986)
  waiting for transfers between devices: 3.75 us -> 9.87 us
  starting transfers between devices: 16.3 us -> 11.4 us
  Pallas kernels: 5.48 us -> 4.64 us
  local copies, waits for them, and re-layouts: 1.67 us -> 1 us
    ppermute x10, waiting for transfers between devices: 3.75 us -> 9.86 us  [across(): return lax.ppermute(block, axis, route)]
    ppermute x10, starting transfers between devices: 14.3 us -> 8.37 us  [across(): return lax.ppermute(block, axis, route)]
    pallas_call x3 -> x1, Pallas kernels: 3.18 us -> 1.21 us  [products(): pl.pallas_call(kernel, out_shape=[out_shape] * len(sides), in_specs=[SMEM...]
    pallas_call x0 -> x3, Pallas kernels: none -> 1.18 us  [the longest x1 0.95 us: own_products(): pl.pallas_call(kernel, out_shape=[jax.ShapeDtypeStruct((RT * tile, tile),...]
    ppermute x2, starting transfers between devices: 2 us -> 3.02 us  [travel(): return lax.ppermute(block, ('row', 'col'), route)]
    unnamed x4 -> x6, local copies, waits for them, and re-layouts: 0.68 us -> 0.01 us
  transfers between devices with their start and end apart: 12 -> 12, of which waited for: 5 -> 5; matrix products, arithmetic and copies ran while one was open for 4% -> 4% of each run, Pallas kernels for 20% -> 17%
where the time goes in v5:
time: 27.9 us; the launch traced here: 27.7 us
  starting transfers between devices  11.4 us (41%)
  waiting for transfers between devices  9.87 us (35%)
  Pallas kernels  4.64 us (17%)
  local copies, waits for them, and re-layouts  1 us (4%)
  other arithmetic  0.71 us (3%)
    ppermute x10, waiting for transfers between devices, across(): return lax.ppermute(block, axis, route)  9.86 us
    ppermute x10, starting transfers between devices, across(): return lax.ppermute(block, axis, route)  8.37 us
    ppermute x2, starting transfers between devices, travel(): return lax.ppermute(block, ('row', 'col'), route)  3.02 us
    pallas_call x1, Pallas kernels, find_matches(): pl.pallas_call(kernel, out_shape=jax.ShapeDtypeStruct((total,), jnp.int32...  2.25 us
    pallas_call x1, Pallas kernels, products(): pl.pallas_call(kernel, out_shape=[out_shape] * len(sides), in_specs=[SMEM...  1.21 us
    squeeze x1, local copies, waits for them, and re-layouts, shards(): given = lax.dynamic_index_in_dim(right, 1 - y, 0, keepdims=False)  0.99 us
    pallas_call x1, Pallas kernels, own_products(): pl.pallas_call(kernel, out_shape=[jax.ShapeDtypeStruct((RT * tile, tile),...  0.95 us
    convert_element_type x1, other arithmetic, shards(): return (mine + decoded(coming) + decoded(from_far)).astype(jnp.bfloat16)  0.69 us
  transfers between devices with their start and end apart: 12, of which 5 were waited for; matrix products, arithmetic and copies ran while one was open for 4% of the time, Pallas kernels for 17%

profile of v5, /device:TPU:0, one launch (start us, length us, event | category | flops | bytes accessed | tf_op | source)
XLA Modules:
  0.0 27.7 jit_solution(3353105318606799506)
XLA Ops:
  0.0 4.0 %collective-permute-start = (bf16[6,128,128]{2,1,0:T(8,128)(2,1)}, bf16[6,128,128]{2,1,0:T(8,128)(2,1)S(1)}, u32[]{:S(2)}, u32[]{:S(2)}) collective-permute-start(bf16[6,128,128]{2,1,0:T(8,128)(2,1)} %bitcast.19), channel_id=1, source_target_pairs={{0,4},{1,5},{2,6},{3,7},{4,0},{5,1},{6,2},{7,3},{8,12},{9,13},{10,... | collective-permute-start | bytes 589832 | tf_op jit(solution)/shard_map/ppermute | solution.py:259
  4.0 0.0 copy-start
  4.0 0.0 copy-start.1
  4.0 0.0 copy-start.2
  4.0 1.0 %dynamic-slice_bitcast_fusion = (bf16[3,128,128]{2,1,0:T(8,128)(2,1)S(1)}, bf16[3,128,128]{2,1,0:T(8,128)(2,1)S(1)}) fusion(bf16[1,1,2,3,128,128]{5,4,3,2,1,0:T(8,128)(2,1)} %param.6, s32[]{:T(128)S(6)} %select_n.8, s32[]{:T(128)S(6)} %select_n.7), kind=kLoop, calls=%fused_computation.5 | loop fusion | bytes 393224 | tf_op jit(solution)/shard_map/jit(dynamic_index_in_dim)/squeeze | solution.py:302
  5.0 1.6 %collective-permute-start.6 = (bf16[3,128,128]{2,1,0:T(8,128)(2,1)S(1)}, bf16[3,128,128]{2,1,0:T(8,128)(2,1)S(1)}, u32[]{:S(2)}, u32[]{:S(2)}) collective-permute-start(bf16[3,128,128]{2,1,0:T(8,128)(2,1)S(1)} %get-tuple-element.29), channel_id=1, source_target_pairs={{1,0},{0,1},{3,2},{2,3},{5,4},{4,5},{13,6},{12,7},{9,8},{8,9},{11,... | collective-permute-start | bytes 294920 | tf_op jit(solution)/shard_map/ppermute | solution.py:269
  6.6 1.4 %collective-permute-start.7 = (bf16[3,128,128]{2,1,0:T(8,128)(2,1)S(1)}, bf16[3,128,128]{2,1,0:T(8,128)(2,1)S(1)}, u32[]{:S(2)}, u32[]{:S(2)}) collective-permute-start(bf16[3,128,128]{2,1,0:T(8,128)(2,1)S(1)} %get-tuple-element.29), channel_id=1, source_target_pairs={{17,0},{16,1},{25,2},{24,3},{21,4},{20,5},{23,6},{22,7},{19,8},{18... | collective-permute-start | bytes 294920 | tf_op jit(solution)/shard_map/ppermute | solution.py:269
  8.1 0.0 copy-done
  8.1 1.1 %collective-permute-start.2 = (bf16[6,128,128]{2,1,0:T(8,128)(2,1)S(1)}, bf16[6,128,128]{2,1,0:T(8,128)(2,1)S(1)}, u32[]{:S(2)}, u32[]{:S(2)}) collective-permute-start(bf16[6,128,128]{2,1,0:T(8,128)(2,1)S(1)} %bitcast.20), channel_id=1, source_target_pairs={{0,2},{1,3},{2,0},{3,1},{4,6},{5,7},{6,4},{7,5},{8,10},{9,11},{10,... | collective-permute-start | bytes 589832 | tf_op jit(solution)/shard_map/ppermute | solution.py:259
  9.2 0.0 collective-permute-start.4
  9.2 0.0 copy-done.1
  9.2 0.0 copy-done.2
  9.2 2.3 %shard_map.46.codes_ref = s32[48]{0:T(128)S(1)} custom-call(s32[6,4,8]{2,1,0:T(4,128)S(1)} %bitcast.23, s32[4,3,2,8]{3,2,1,0:T(2,128)S(1)} %bitcast.24), custom_call_target="tpu_custom_call" | custom-call | tf_op jit(solution)/shard_map/pallas_call | solution.py:62
  11.5 2.0 %collective-permute-done.refs_2_ = bf16[6,128,128]{2,1,0:T(8,128)(2,1)S(1)} collective-permute-done((bf16[6,128,128]{2,1,0:T(8,128)(2,1)}, bf16[6,128,128]{2,1,0:T(8,128)(2,1)S(1)}, u32[]{:S(2)}, u32[]{:S(2)}) %collective-permute-start) | collective-permute-done | bytes 196640 | tf_op jit(solution)/shard_map/ppermute | solution.py:259
  13.5 0.8 %collective-permute-start.1 = (bf16[6,128,128]{2,1,0:T(8,128)(2,1)S(1)}, bf16[6,128,128]{2,1,0:T(8,128)(2,1)S(1)}, u32[]{:S(2)}, u32[]{:S(2)}) collective-permute-start(bf16[6,128,128]{2,1,0:T(8,128)(2,1)S(1)} %collective-permute-done.refs_2_), channel_id=1, source_target_pairs={{0,2},{1,3},{2,0},{3,1},{4,6},{5,7},{6,4},{7,5},{8,10},{9,11},{10,... | collective-permute-start | bytes 589832 | tf_op jit(solution)/shard_map/ppermute | solution.py:259
  14.2 0.0 collective-permute-done.6.refs_0_
  14.2 0.0 collective-permute-done.7.refs_1_
  14.3 0.1 collective-permute-start.8
  14.3 0.5 %collective-permute-start.9 = (bf16[3,128,128]{2,1,0:T(8,128)(2,1)S(1)}, bf16[3,128,128]{2,1,0:T(8,128)(2,1)S(1)}, u32[]{:S(2)}, u32[]{:S(2)}) collective-permute-start(bf16[3,128,128]{2,1,0:T(8,128)(2,1)S(1)} %get-tuple-element.31.refs_8_), channel_id=1, source_target_pairs={{0,8},{8,0},{16,24},{24,16},{1,9},{9,1},{17,25},{25,17},{2,10},{10... | collective-permute-start | bytes 294920 | tf_op jit(solution)/shard_map/ppermute | solution.py:259
  14.8 0.0 collective-permute-done.4.refs_5_.refs_7_
  14.8 0.1 collective-permute-start.5
  14.9 2.7 %collective-permute-done.2.refs_1_ = bf16[6,128,128]{2,1,0:T(8,128)(2,1)S(1)} collective-permute-done((bf16[6,128,128]{2,1,0:T(8,128)(2,1)S(1)}, bf16[6,128,128]{2,1,0:T(8,128)(2,1)S(1)}, u32[]{:S(2)}, u32[]{:S(2)}) %collective-permute-start.2) | collective-permute-done | bytes 196640 | tf_op jit(solution)/shard_map/ppermute | solution.py:259
  17.6 0.1 collective-permute-start.3
  17.7 0.0 collective-permute-done.8.refs_6_
  17.7 0.0 collective-permute-done.9.refs_10_
  17.7 0.0 collective-permute-done.5.refs_6_.refs_9_
  17.7 1.2 %collective-permute-done.3.refs_4_.refs_5_ = bf16[3,128,128]{2,1,0:T(8,128)(2,1)S(1)} collective-permute-done((bf16[3,128,128]{2,1,0:T(8,128)(2,1)S(1)}, bf16[3,128,128]{2,1,0:T(8,128)(2,1)S(1)}, u32[]{:S(2)}, u32[]{:S(2)}) %collective-permute-start.3) | collective-permute-done | bytes 98336 | tf_op jit(solution)/shard_map/ppermute | solution.py:259
  18.9 1.2 %shard_map.50 = (s16[272,128]{1,0:T(8,128)(2,1)S(1)}, s16[272,128]{1,0:T(8,128)(2,1)S(1)}) custom-call(s32[48]{0:T(128)S(1)} %shard_map.46.codes_ref, bf16[6,128,128]{2,1,0:T(8,128)(2,1)S(1)} %bitcast.21, bf16[6,128,128]{2,1,0:T(8,128)(2,1)S(1)} %collective-permute-done.2.refs_1_, bf16[6,128,128]{2,1,0:T(8,128)(2,1)S(1)} %collective-permute-done.refs_2_, ...), custom_call_target="tpu_custom_call" | custom-call | flops 100000000 | bytes 589824 | tf_op jit(solution)/shard_map/pallas_call | solution.py:118
  20.1 1.7 %collective-permute-start.10 = (s16[272,128]{1,0:T(8,128)(2,1)S(1)}, s16[272,128]{1,0:T(8,128)(2,1)S(1)}, u32[]{:S(2)}, u32[]{:S(2)}) collective-permute-start(s16[272,128]{1,0:T(8,128)(2,1)S(1)} %get-tuple-element.32), channel_id=1, source_target_pairs={{0,1},{1,0},{2,3},{3,2},{4,5},{5,4},{6,7},{7,6},{8,9},{9,8},{10,11... | collective-permute-start | bytes 208904 | tf_op jit(solution)/shard_map/ppermute | solution.py:259
  21.8 0.0 collective-permute-start.11
  21.8 0.9 %shard_map.47 = (f32[256,128]{1,0:T(8,128)S(1)}, bf16[1,768,256]{2,1,0:T(8,128)(2,1)S(1)}) custom-call(s32[48]{0:T(128)S(1)} %shard_map.46.codes_ref, bf16[6,128,128]{2,1,0:T(8,128)(2,1)S(1)} %bitcast.22, bf16[6,128,128]{2,1,0:T(8,128)(2,1)S(1)} %collective-permute-done.2.refs_1_, bf16[6,128,128]{2,1,0:T(8,128)(2,1)S(1)} %collective-permute-done.refs_2_, ...), custom_call_target="tpu_custom_call" | custom-call | flops 100000000 | bytes 196608 | tf_op jit(solution)/shard_map/pallas_call | solution.py:174
  22.7 0.0 collective-permute-done.1.refs_0_
  22.7 0.2 shard_map.48
  23.0 2.4 %collective-permute-done.10 = s16[272,128]{1,0:T(8,128)(2,1)S(1)} collective-permute-done((s16[272,128]{1,0:T(8,128)(2,1)S(1)}, s16[272,128]{1,0:T(8,128)(2,1)S(1)}, u32[]{:S(2)}, u32[]{:S(2)}) %collective-permute-start.10) | collective-permute-done | bytes 69664 | tf_op jit(solution)/shard_map/ppermute | solution.py:259
  25.4 1.6 %collective-permute-done.11 = s16[272,128]{1,0:T(8,128)(2,1)S(1)} collective-permute-done((s16[272,128]{1,0:T(8,128)(2,1)S(1)}, s16[272,128]{1,0:T(8,128)(2,1)S(1)}, u32[]{:S(2)}, u32[]{:S(2)}) %collective-permute-start.11) | collective-permute-done | bytes 69664 | tf_op jit(solution)/shard_map/ppermute | solution.py:259
  27.0 0.7 %fusion.1 = bf16[256,128]{1,0:T(8,128)(2,1)} fusion(f32[256,128]{1,0:T(8,128)S(1)} %shard_map.48, f32[2,128]{1,0:T(2,128)S(1)} %get-tuple-element.39, s16[272,128]{1,0:T(8,128)(2,1)S(1)} %collective-permute-done.11, f32[2,128]{1,0:T(2,128)S(1)} %get-tuple-element.40, s16[272,128]{1,0:T(8,128)(2,1)S(1)} %collective-permute-done.10), kind=kLoop, calls=%fused_computation.2 | loop fusion | flops 229376 | bytes 329728 | tf_op jit(solution)/shard_map/convert_element_type | solution.py:323
  (2 shorter events, 0.0 us)
Async XLA Ops:
  0.0 13.5 %collective-permute-start = (bf16[6,128,128]{2,1,0:T(8,128)(2,1)}, bf16[6,128,128]{2,1,0:T(8,128)(2,1)S(1)}, u32[]{:S(2)}, u32[]{:S(2)}) collective-permute-start(bf16[6,128,128]{2,1,0:T(8,128)(2,1)} %bitcast.19), channel_id=1, source_target_pairs={{0,4},{1,5},{2,6},{3,7},{4,0},{5,1},{6,2},{7,3},{8,12},{9,13},{10,... | collective-permute-start | bytes 589832 | tf_op jit(solution)/shard_map/ppermute | solution.py:259
  4.0 4.0 %copy-start = (bf16[1,1,6,128,128]{4,3,2,1,0:T(8,128)(2,1)S(1)}, bf16[1,1,6,128,128]{4,3,2,1,0:T(8,128)(2,1)}, u32[]{:S(2)}) copy-start(bf16[1,1,6,128,128]{4,3,2,1,0:T(8,128)(2,1)} %param.4) | copy-start | bytes 589828
  4.0 5.2 %copy-start.1 = (s32[4,8,6]{1,0,2:T(4,128)S(1)}, s32[4,8,6]{1,0,2:T(4,128)}, u32[]{:S(2)}) copy-start(s32[4,8,6]{1,0,2:T(4,128)} %param.5) | copy-start | bytes 2308
  4.0 5.2 %copy-start.2 = (s32[4,8,2,3]{1,2,3,0:T(2,128)S(1)}, s32[4,8,2,3]{1,2,3,0:T(2,128)}, u32[]{:S(2)}) copy-start(s32[4,8,2,3]{1,2,3,0:T(2,128)} %param.7) | copy-start | bytes 2308
  5.0 9.2 %collective-permute-start.6 = (bf16[3,128,128]{2,1,0:T(8,128)(2,1)S(1)}, bf16[3,128,128]{2,1,0:T(8,128)(2,1)S(1)}, u32[]{:S(2)}, u32[]{:S(2)}) collective-permute-start(bf16[3,128,128]{2,1,0:T(8,128)(2,1)S(1)} %get-tuple-element.29), channel_id=1, source_target_pairs={{1,0},{0,1},{3,2},{2,3},{5,4},{4,5},{13,6},{12,7},{9,8},{8,9},{11,... | collective-permute-start | bytes 294920 | tf_op jit(solution)/shard_map/ppermute | solution.py:269
  6.6 7.6 %collective-permute-start.7 = (bf16[3,128,128]{2,1,0:T(8,128)(2,1)S(1)}, bf16[3,128,128]{2,1,0:T(8,128)(2,1)S(1)}, u32[]{:S(2)}, u32[]{:S(2)}) collective-permute-start(bf16[3,128,128]{2,1,0:T(8,128)(2,1)S(1)} %get-tuple-element.29), channel_id=1, source_target_pairs={{17,0},{16,1},{25,2},{24,3},{21,4},{20,5},{23,6},{22,7},{19,8},{18... | collective-permute-start | bytes 294920 | tf_op jit(solution)/shard_map/ppermute | solution.py:269
  8.1 9.5 %collective-permute-start.2 = (bf16[6,128,128]{2,1,0:T(8,128)(2,1)S(1)}, bf16[6,128,128]{2,1,0:T(8,128)(2,1)S(1)}, u32[]{:S(2)}, u32[]{:S(2)}) collective-permute-start(bf16[6,128,128]{2,1,0:T(8,128)(2,1)S(1)} %bitcast.20), channel_id=1, source_target_pairs={{0,2},{1,3},{2,0},{3,1},{4,6},{5,7},{6,4},{7,5},{8,10},{9,11},{10,... | collective-permute-start | bytes 589832 | tf_op jit(solution)/shard_map/ppermute | solution.py:259
  9.2 5.6 %collective-permute-start.4 = (bf16[3,128,128]{2,1,0:T(8,128)(2,1)S(1)}, bf16[3,128,128]{2,1,0:T(8,128)(2,1)S(1)}, u32[]{:S(2)}, u32[]{:S(2)}) collective-permute-start(bf16[3,128,128]{2,1,0:T(8,128)(2,1)S(1)} %get-tuple-element.26.refs_3_), channel_id=1, source_target_pairs={{0,16},{8,24},{16,0},{24,8},{1,17},{9,25},{17,1},{25,9},{2,18},{10... | collective-permute-start | bytes 294920 | tf_op jit(solution)/shard_map/ppermute | solution.py:259
  13.5 9.3 %collective-permute-start.1 = (bf16[6,128,128]{2,1,0:T(8,128)(2,1)S(1)}, bf16[6,128,128]{2,1,0:T(8,128)(2,1)S(1)}, u32[]{:S(2)}, u32[]{:S(2)}) collective-permute-start(bf16[6,128,128]{2,1,0:T(8,128)(2,1)S(1)} %collective-permute-done.refs_2_), channel_id=1, source_target_pairs={{0,2},{1,3},{2,0},{3,1},{4,6},{5,7},{6,4},{7,5},{8,10},{9,11},{10,... | collective-permute-start | bytes 589832 | tf_op jit(solution)/shard_map/ppermute | solution.py:259
  14.3 3.4 %collective-permute-start.8 = (bf16[3,128,128]{2,1,0:T(8,128)(2,1)S(1)}, bf16[3,128,128]{2,1,0:T(8,128)(2,1)S(1)}, u32[]{:S(2)}, u32[]{:S(2)}) collective-permute-start(bf16[3,128,128]{2,1,0:T(8,128)(2,1)S(1)} %get-tuple-element.30.refs_4_), channel_id=1, source_target_pairs={{0,8},{8,0},{16,24},{24,16},{1,9},{9,1},{17,25},{25,17},{2,10},{10... | collective-permute-start | bytes 294920 | tf_op jit(solution)/shard_map/ppermute | solution.py:259
  14.3 3.3 %collective-permute-start.9 = (bf16[3,128,128]{2,1,0:T(8,128)(2,1)S(1)}, bf16[3,128,128]{2,1,0:T(8,128)(2,1)S(1)}, u32[]{:S(2)}, u32[]{:S(2)}) collective-permute-start(bf16[3,128,128]{2,1,0:T(8,128)(2,1)S(1)} %get-tuple-element.31.refs_8_), channel_id=1, source_target_pairs={{0,8},{8,0},{16,24},{24,16},{1,9},{9,1},{17,25},{25,17},{2,10},{10... | collective-permute-start | bytes 294920 | tf_op jit(solution)/shard_map/ppermute | solution.py:259
  14.8 2.8 %collective-permute-start.5 = (bf16[3,128,128]{2,1,0:T(8,128)(2,1)S(1)}, bf16[3,128,128]{2,1,0:T(8,128)(2,1)S(1)}, u32[]{:S(2)}, u32[]{:S(2)}) collective-permute-start(bf16[3,128,128]{2,1,0:T(8,128)(2,1)S(1)} %collective-permute-done.4.refs_5_.refs_7_), channel_id=1, source_target_pairs={{0,8},{8,0},{16,24},{24,16},{1,9},{9,1},{17,25},{25,17},{2,10},{10... | collective-permute-start | bytes 294920 | tf_op jit(solution)/shard_map/ppermute | solution.py:259
  17.6 1.3 %collective-permute-start.3 = (bf16[3,128,128]{2,1,0:T(8,128)(2,1)S(1)}, bf16[3,128,128]{2,1,0:T(8,128)(2,1)S(1)}, u32[]{:S(2)}, u32[]{:S(2)}) collective-permute-start(bf16[3,128,128]{2,1,0:T(8,128)(2,1)S(1)} %get-tuple-element.26.refs_3_), channel_id=1, source_target_pairs={{0,8},{8,0},{16,24},{24,16},{1,9},{9,1},{17,25},{25,17},{2,10},{10... | collective-permute-start | bytes 294920 | tf_op jit(solution)/shard_map/ppermute | solution.py:259
  20.1 5.3 %collective-permute-start.10 = (s16[272,128]{1,0:T(8,128)(2,1)S(1)}, s16[272,128]{1,0:T(8,128)(2,1)S(1)}, u32[]{:S(2)}, u32[]{:S(2)}) collective-permute-start(s16[272,128]{1,0:T(8,128)(2,1)S(1)} %get-tuple-element.32), channel_id=1, source_target_pairs={{0,1},{1,0},{2,3},{3,2},{4,5},{5,4},{6,7},{7,6},{8,9},{9,8},{10,11... | collective-permute-start | bytes 208904 | tf_op jit(solution)/shard_map/ppermute | solution.py:259
  21.8 5.2 %collective-permute-start.11 = (s16[272,128]{1,0:T(8,128)(2,1)S(1)}, s16[272,128]{1,0:T(8,128)(2,1)S(1)}, u32[]{:S(2)}, u32[]{:S(2)}) collective-permute-start(s16[272,128]{1,0:T(8,128)(2,1)S(1)} %get-tuple-element.33), channel_id=1, source_target_pairs={{0,3},{1,2},{2,1},{3,0},{4,7},{5,6},{6,5},{7,4},{8,11},{9,10},{10,... | collective-permute-start | bytes 208904 | tf_op jit(solution)/shard_map/ppermute | solution.py:259
